TPU v7x, 512 devices: a whole 4x4x16 slice. The times are simulated.
512 devices in a mesh: depth: 8 (over y, core), row: 4 (over x), col: 16 (over z).
Axes of the slice: x: 4, y: 4, z: 16, core: 2. Of those that a mesh axis runs over, the one named last changes fastest.
Arguments:
- grad_out: bfloat16 [4096, 8192], P('depth', ('row', 'col')), may hold values from -16 to 16
- gate_pre: bfloat16 [4096, 14336], P('depth', ('row', 'col')), may hold values from -6 to 6
- up_pre: bfloat16 [4096, 14336], P('depth', ('row', 'col')), may hold values from -6 to 6
- down_weight: bfloat16 [14336, 8192], P(('row', 'col')), may hold values from -0.0625 to 0.0625
Outputs:
- grad_gate: bfloat16 [4096, 14336], P('depth', ('row', 'col'))
- grad_up: bfloat16 [4096, 14336], P('depth', ('row', 'col'))
- grad_down: bfloat16 [14336, 8192], P(('row', 'col'), 'depth')
All inputs are finite; a program needn't handle non-finite values.
Results may differ from a plain program's by a relative error of at most 0.017.
Values may be sent and summed in bfloat16 or wider, within the bound.
No kernel may reach another device: no remote copies, remote signals or barrier semaphores. Data moves between devices by JAX's collectives and lax.ppermute only.
A program may use at most 64 MiB of HBM per device.

v0:
```python
import jax
import jax.numpy as jnp
from jax import lax
from jax.sharding import PartitionSpec as P


def shards(grad_out, gate_pre, up_pre, down_weight):
    gate = gate_pre.astype(jnp.float32)
    upval = up_pre.astype(jnp.float32)
    sigma = jax.nn.sigmoid(gate)
    active = gate * sigma
    hidden = (active * upval).astype(jnp.bfloat16)
    tok_rows = grad_out.shape[0]
    scale = 1.0 / jnp.sqrt(jnp.float32(tok_rows * lax.axis_size("depth")))
    piece = lax.all_gather(grad_out, ("row", "col"), axis=1, tiled=True)
    grad_hidden = lax.dot_general(
        piece, down_weight, (((1,), (1,)), ((), ())), preferred_element_type=jnp.float32
    )
    block = lax.dot_general(
        hidden, piece, (((0,), (0,)), ((), ())), preferred_element_type=jnp.float32
    )
    weight_term = block
    grad_hidden, weight_term = (grad_hidden, weight_term)
    grad_up = (grad_hidden * active).astype(jnp.bfloat16)
    grad_gate = (grad_hidden * upval * sigma * (1.0 + gate * (1.0 - sigma))).astype(jnp.bfloat16)
    grad_down = lax.psum_scatter(
        (weight_term * scale).astype(jnp.bfloat16), "depth", scatter_dimension=1, tiled=True
    )
    return (grad_gate, grad_up, grad_down)


def solution(mesh):
    in_specs = (
        P("depth", ("row", "col")),
        P("depth", ("row", "col")),
        P("depth", ("row", "col")),
        P(("row", "col"), None),
    )
    out_specs = (P("depth", ("row", "col")), P("depth", ("row", "col")), P(("row", "col"), "depth"))
    return jax.shard_map(shards, mesh=mesh, in_specs=in_specs, out_specs=out_specs, check_vma=False)
```

profile of v0, /device:TPU:7, one launch (start us, length us, event | category | flops | bytes accessed | tf_op | source)
XLA Modules:
  0.0 234.2 jit_solution(15545076601416861504)
XLA Ops:
  7.2 0.0 all-gather.2.cloned.1.call-start
  7.2 0.7 all-gather.2.cloned.1.call-update
  7.9 0.0 copy-start
  7.9 0.0 copy-start.1
  7.9 0.0 reduce-scatter.2.cloned.1.call-start
  8.0 164.3 %all-gather.2.cloned.1.call-done = bf16[512,8192]{1,0:T(8,128)(2,1)} async-done(((bf16[512,128]{1,0:T(8,128)(2,1)}), bf16[512,8192]{1,0:T(8,128)(2,1)}) %all-gather.2.cloned.1.call-update) | async-done | bytes 8388624 | tf_op jit(solution)/shard_map/all_gather | solution.py:15
  172.3 7.6 %fusion = bf16[224,8192]{1,0:T(8,128)(2,1)} fusion(bf16[512,8192]{1,0:T(8,128)(2,1)} %all-gather.2.cloned.1.call-done, bf16[512,224]{0,1:T(8,128)(2,1)} %param.6, bf16[512,224]{0,1:T(8,128)(2,1)} %param.5), kind=kOutput, calls=%fused_computation.1 | convolution fusion | flops 1883635712 | bytes 12517376 | tf_op jit(solution)/shard_map/dot_general | solution.py:19
  179.9 0.0 reduce-scatter.2.cloned.1.call-update
  179.9 0.0 copy-done
  179.9 0.0 copy-done.1
  179.9 8.0 %multiply_convert_fusion = (bf16[512,224]{0,1:T(8,128)(2,1)}, bf16[512,224]{0,1:T(8,128)(2,1)}) fusion(bf16[512,224]{0,1:T(8,128)(2,1)S(1)} %copy-done, bf16[512,224]{0,1:T(8,128)(2,1)S(1)} %copy-done.1, bf16[512,8192]{1,0:T(8,128)(2,1)} %all-gather.2.cloned.1.call-done, bf16[224,8192]{1,0:T(8,128)(2,1)} %param.7), kind=kOutput, calls=%fused_computation.15 | convolution fusion | flops 1880768512 | bytes 12976128 | tf_op jit(solution)/shard_map/dot_general | solution.py:16
  187.9 39.4 %reduce-scatter.2.cloned.1.call-done = bf16[224,1024]{1,0:T(8,128)(2,1)} async-done(((bf16[224,8192]{1,0:T(8,128)(2,1)}), bf16[224,1024]{1,0:T(8,128)(2,1)}) %reduce-scatter.2.cloned.1.call-update) | async-done | bytes 458768 | tf_op jit(solution)/shard_map/reduce_scatter | solution.py:26
Async XLA Ops:
  7.2 165.1 %all-gather.2.cloned.1.call-start = ((), (), s32[]{:S(2)}) async-start(), calls=%async_computation.1 | async-start | bytes 8519680 | tf_op jit(solution)/shard_map/all_gather | solution.py:15
  7.9 172.0 %copy-start = (bf16[512,224]{0,1:T(8,128)(2,1)S(1)}, bf16[512,224]{0,1:T(8,128)(2,1)}, u32[]{:S(2)}) copy-start(bf16[512,224]{0,1:T(8,128)(2,1)} %param.5) | copy-start | bytes 688132
  7.9 172.0 %copy-start.1 = (bf16[512,224]{0,1:T(8,128)(2,1)S(1)}, bf16[512,224]{0,1:T(8,128)(2,1)}, u32[]{:S(2)}) copy-start(bf16[512,224]{0,1:T(8,128)(2,1)} %param.6) | copy-start | bytes 688132
  7.9 219.4 %reduce-scatter.2.cloned.1.call-start = ((), (), s32[]{:S(2)}) async-start(), calls=%async_computation.2 | async-start | bytes 4128768 | tf_op jit(solution)/shard_map/reduce_scatter | solution.py:26
Sparse Core Ops, SparseCore 0:
  10.9 161.3 all-gather.1
  180.0 47.2 reduce-scatter.1
where the time goes:
time: 237 us; the launch traced here: 234 us
  waiting for transfers between devices  204 us (86%)
  matrix products  15.6 us (7%)
  between operations  14.1 us (6%)
    all_gather x1, waiting for transfers between devices, shards(): piece = lax.all_gather(grad_out, ('row', 'col'), axis=1, tiled=True)  164 us
    reduce_scatter x1, waiting for transfers between devices, shards(): lax.psum_scatter((weight_term * scale).astype(jnp.bfloat16), 'depth', sca...  39.4 us
    dot_general x1, matrix products, shards(): lax.dot_general(piece, down_weight, (((1,), (1,)), ((), ())), preferred_e...  7.99 us
    dot_general x1, matrix products, shards(): lax.dot_general(hidden, piece, (((0,), (0,)), ((), ())), preferred_elemen...  7.63 us
  transfers between devices with their start and end apart: 2, of which 2 were waited for; matrix products, arithmetic and copies ran while one was open for 3% of the time, Pallas kernels for 0%

commit v1 on v0

v1 whole, which is shorter than its diff:
```python
import jax
import jax.numpy as jnp
from jax import lax
from jax.experimental import pallas as pl
from jax.experimental.pallas import tpu as pltpu
from jax.sharding import PartitionSpec as P

ZG = [[g + 4 * j for j in range(4)] for g in range(4)]
YS = [[0, 2, 4, 6], [1, 3, 5, 7]]


def from_col(a, k):
    return lax.ppermute(a, "col", [((i + k) % 16, i) for i in range(16)])


def other_core(a):
    return lax.ppermute(a, "depth", [(i, i ^ 1) for i in range(8)])


def wide(ref):
    return jnp.concatenate([ref[0], ref[1]], axis=1)


def partial_kernel(pos, hid, s0, s1, s2, s3, out):
    rows = hid.shape[0] * hid.shape[1]
    h = hid[...].reshape(rows, hid.shape[2])
    for r, s in enumerate((s0, s1, s2, s3)):
        p = jnp.dot(h, wide(s), preferred_element_type=jnp.float32) * (1.0 / 64.0)
        out[:, :, r * 256 : r * 256 + 256] = p.astype(out.dtype).reshape(hid.shape[0], hid.shape[1], 256)


def partial_add_kernel(pos, hid, s0, s1, s2, s3, got, out):
    rows = hid.shape[0] * hid.shape[1]
    h = hid[...].reshape(rows, hid.shape[2])
    for r, s in enumerate((s0, s1, s2, s3)):
        p = jnp.dot(h, wide(s), preferred_element_type=jnp.float32) * (1.0 / 64.0)
        q = p.reshape(hid.shape[0], hid.shape[1], 256) + got[:, :, r * 256 : r * 256 + 256].astype(jnp.float32)
        out[:, :, r * 256 : r * 256 + 256] = q.astype(out.dtype)


def partial_call(pos, which, hid, sets, got=None):
    n, f, t = hid.shape
    whole = lambda shape: pl.BlockSpec(shape, lambda i, p: (0,) * len(shape))
    half = pl.BlockSpec((2, t, 128), lambda i, p: (p[which], 0, 0))
    specs = [whole((n, f, t))] + [half] * 4 + ([whole((n, f, 1024))] if got is not None else [])
    args = [hid, *sets] + ([got] if got is not None else [])
    return pl.pallas_call(
        partial_kernel if got is None else partial_add_kernel,
        grid_spec=pltpu.PrefetchScalarGridSpec(
            num_scalar_prefetch=1, grid=(1,), in_specs=specs, out_specs=whole((n, f, 1024))
        ),
        out_shape=jax.ShapeDtypeStruct((n, f, 1024), jnp.bfloat16),
        compiler_params=pltpu.CompilerParams(vmem_limit_bytes=48 * 1024 * 1024),
        cost_estimate=pl.CostEstimate(flops=2 * n * f * t * 1024, bytes_accessed=4 * 1024 * 1024, transcendentals=0),
    )(pos, *args)


def hidden_grad_kernel(pos, wa, wb, a0, a1, a2, a3, b0, b1, b2, b3, out, acc, cat):
    i = pl.program_id(0)
    zl = pos[2]
    rows = wa.shape[0] * wa.shape[1]
    total = None
    for r in range(4):
        at = pl.multiple_of(lax.rem(zl + r, 4) * 128, 128)
        cat[0, :, pl.ds(at, 128)] = (a0, a1, a2, a3)[r][0]
        cat[1, :, pl.ds(at, 128)] = (b0, b1, b2, b3)[r][0]
    for k, w in enumerate((wa, wb)):
        part = lax.dot_general(
            w[...].reshape(rows, w.shape[2]), cat[k], (((1,), (1,)), ((), ())), preferred_element_type=jnp.float32
        )
        total = part if total is None else total + part

    @pl.when(i == 0)
    def _():
        acc[...] = total

    @pl.when(i == 1)
    def _():
        out[...] = (acc[...] + total).astype(out.dtype).reshape(out.shape)


def hidden_grad_call(pos, wa, wb, sets):
    n, f, _ = wa.shape
    t = sets[0].shape[1]
    wspec = pl.BlockSpec((n, f, 512), lambda i, p: (0, 0, i))
    mine = pl.BlockSpec((1, t, 128), lambda i, p: (2 * p[0] + i, 0, 0))
    others = pl.BlockSpec((1, t, 128), lambda i, p: (2 * p[1] + i, 0, 0))
    return pl.pallas_call(
        hidden_grad_kernel,
        grid_spec=pltpu.PrefetchScalarGridSpec(
            num_scalar_prefetch=1,
            grid=(2,),
            in_specs=[wspec, wspec] + [mine] * 4 + [others] * 4,
            out_specs=pl.BlockSpec((n, f, t), lambda i, p: (0, 0, 0)),
            scratch_shapes=[pltpu.VMEM((n * f, t), jnp.float32), pltpu.VMEM((2, t, 512), jnp.bfloat16)],
        ),
        out_shape=jax.ShapeDtypeStruct((n, f, t), jnp.bfloat16),
        compiler_params=pltpu.CompilerParams(vmem_limit_bytes=48 * 1024 * 1024),
        cost_estimate=pl.CostEstimate(flops=2 * n * f * t * 2048, bytes_accessed=7 * 1024 * 1024, transcendentals=0),
    )(pos, wa, wb, *sets, *sets)


def sum_kernel(pos, q, out):
    zl = pos[2]
    for r in range(4):
        for k in range(2):
            lo = r * 256 + k * 128
            s = q[0, :, lo : lo + 128].astype(jnp.float32)
            for y in range(1, 4):
                s = s + q[y, :, lo : lo + 128].astype(jnp.float32)
            at = pl.multiple_of(k * 512 + lax.rem(zl + r, 4) * 128, 128)
            out[:, pl.ds(at, 128)] = s.astype(out.dtype)


def sum_call(pos, q):
    n, f, d = q.shape
    return pl.pallas_call(
        sum_kernel,
        grid_spec=pltpu.PrefetchScalarGridSpec(
            num_scalar_prefetch=1,
            grid=(1,),
            in_specs=[pl.BlockSpec((n, f, d), lambda i, p: (0, 0, 0))],
            out_specs=pl.BlockSpec((f, d), lambda i, p: (0, 0)),
        ),
        out_shape=jax.ShapeDtypeStruct((f, d), jnp.bfloat16),
        compiler_params=pltpu.CompilerParams(vmem_limit_bytes=32 * 1024 * 1024),
        cost_estimate=pl.CostEstimate(flops=n * f * d, bytes_accessed=5 * f * d * 2, transcendentals=0),
    )(pos, q)


def shards(grad_out, gate_pre, up_pre, down_weight):
    depth, row, col = lax.axis_index("depth"), lax.axis_index("row"), lax.axis_index("col")
    core = depth % 2
    zl = col % 4
    pos = jnp.stack([core, 1 - core, zl]).astype(jnp.int32)
    f = down_weight.shape[0]

    gate = gate_pre.T.astype(jnp.float32)
    upval = up_pre.T.astype(jnp.float32)
    sigma = jax.nn.sigmoid(gate)
    active = gate * sigma
    hidden = (active * upval).astype(jnp.bfloat16)

    hid = lax.all_to_all(jnp.broadcast_to(hidden[None], (4,) + hidden.shape), "row", 0, 0)
    hid = lax.dynamic_slice_in_dim(jnp.concatenate([hid, hid]), (4 - row) % 4, 4, 0)

    wcols = lax.dynamic_index_in_dim(down_weight.reshape(f, 4, 2, 1024), core, 2, keepdims=False)
    wa = lax.all_to_all(wcols.transpose(1, 0, 2), "row", 0, 0)
    wb = other_core(wa)

    set0 = lax.all_gather(grad_out, "col", axis=0, axis_index_groups=ZG)
    set1 = from_col(set0, 1)
    set3 = from_col(set0, -1)
    set2 = jnp.concatenate([from_col(set0[:2], 2), from_col(set0[2:], -2)])
    sets = (set0, set1, set2, set3)

    away = partial_call(pos, 1, hid, sets)
    both = partial_call(pos, 0, hid, sets, other_core(away))
    parts = lax.all_to_all(both, "depth", 0, 0, axis_index_groups=YS)
    total = sum_call(pos, parts)
    perm = []
    for y in range(4):
        for c in range(2):
            for x in range(4):
                perm.append(((2 * y + c) * 4 + x, (2 * x + c) * 4 + (y - x) % 4))
    grad_down = lax.ppermute(total, ("depth", "row"), perm)

    terms = lax.all_to_all(hidden_grad_call(pos, wa, wb, sets), "row", 0, 0)
    grad_hidden = terms.astype(jnp.float32).sum(0)
    grad_up = (grad_hidden * active).astype(jnp.bfloat16)
    grad_gate = (grad_hidden * upval * sigma * (1.0 + gate * (1.0 - sigma))).astype(jnp.bfloat16)
    return (grad_gate.T, grad_up.T, grad_down)


def solution(mesh):
    in_specs = (
        P("depth", ("row", "col")),
        P("depth", ("row", "col")),
        P("depth", ("row", "col")),
        P(("row", "col"), None),
    )
    out_specs = (P("depth", ("row", "col")), P("depth", ("row", "col")), P(("row", "col"), "depth"))
    return jax.shard_map(shards, mesh=mesh, in_specs=in_specs, out_specs=out_specs, check_vma=False)
```

time: 237 us -> 164 us (0.69)
  waiting for transfers between devices: 204 us -> 37.3 us
  starting transfers between devices: 0.08 us -> 49.4 us
  blocking collectives: 0 us -> 30.7 us
  local copies, waits for them, and re-layouts: 0.01 us -> 27.4 us
  matrix products: 15.6 us -> 0 us
  Pallas kernels: 0 us -> 14.5 us
  between operations: 14.1 us -> 0.83 us
  other arithmetic: 0 us -> 2.84 us
    all_gather x1 -> x0, waiting for transfers between devices: 164 us -> none  [shards(): piece = lax.all_gather(grad_out, ('row', 'col'), axis=1, tiled=True)]
    reduce_scatter x1 -> x0, waiting for transfers between devices: 39.4 us -> none  [shards(): lax.psum_scatter((weight_term * scale).astype(jnp.bfloat16), 'depth', sca...]
    ppermute x0 -> x7, starting transfers between devices: none -> 31.2 us  [the longest x2 16.1 us: other_core(): return lax.ppermute(a, 'depth', [(i, i ^ 1) for i in range(8)])]
    all_gather x0 -> x1, blocking collectives: none -> 30.7 us  [shards(): set0 = lax.all_gather(grad_out, 'col', axis=0, axis_index_groups=ZG)]
    all_to_all x0 -> x4, waiting for transfers between devices: none -> 26.7 us  [the longest x1 17.5 us: shards(): parts = lax.all_to_all(both, 'depth', 0, 0, axis_index_groups=YS)]
    all_to_all x0 -> x4, starting transfers between devices: none -> 18.2 us  [the longest x1 5.23 us: shards(): terms = lax.all_to_all(hidden_grad_call(pos, wa, wb, sets), 'row', 0, 0)]
    dot_general x2 -> x0, matrix products: 15.6 us -> none  [the longest x1 7.99 us: shards(): lax.dot_general(piece, down_weight, (((1,), (1,)), ((), ())), preferred_e...]
    pallas_call x0 -> x4, Pallas kernels: none -> 14.5 us  [the longest x2 6.11 us: partial_call(): pl.pallas_call(partial_kernel if got is None else partial_add_kernel, gri...]
  transfers between devices with their start and end apart: 2 -> 11, of which waited for: 2 -> 4; matrix products, arithmetic and copies ran while one was open for 3% -> 17% of each run, Pallas kernels for 0% -> 9%
where the time goes in v1:
time: 164 us; the launch traced here: 163 us
  starting transfers between devices  49.4 us (30%)
  waiting for transfers between devices  37.3 us (23%)
  blocking collectives  30.7 us (19%)
  local copies, waits for them, and re-layouts  27.4 us (17%)
  Pallas kernels  14.5 us (9%)
  other arithmetic  2.84 us (2%)
    all_gather x1, blocking collectives, shards(): set0 = lax.all_gather(grad_out, 'col', axis=0, axis_index_groups=ZG)  30.7 us
    all_to_all x1, waiting for transfers between devices, shards(): parts = lax.all_to_all(both, 'depth', 0, 0, axis_index_groups=YS)  17.5 us
    ppermute x2, starting transfers between devices, other_core(): return lax.ppermute(a, 'depth', [(i, i ^ 1) for i in range(8)])  16.1 us
    ppermute x4, starting transfers between devices, from_col(): return lax.ppermute(a, 'col', [((i + k) % 16, i) for i in range(16)])  11.4 us
    ppermute x1, waiting for transfers between devices, shards(): grad_down = lax.ppermute(total, ('depth', 'row'), perm)  10.7 us
    unnamed x11, local copies, waits for them, and re-layouts  9.17 us
    dynamic_slice x1, local copies, waits for them, and re-layouts, shards(): lax.dynamic_index_in_dim(down_weight.reshape(f, 4, 2, 1024), core, 2, kee...  8.32 us
    reshape x1, local copies, waits for them, and re-layouts, shards(): down_weight.reshape(f, 4, 2, 1024)  7.14 us
  transfers between devices with their start and end apart: 11, of which 4 were waited for; matrix products, arithmetic and copies ran while one was open for 17% of the time, Pallas kernels for 9%

profile of v1, /device:TPU:7, one launch (start us, length us, event | category | flops | bytes accessed | tf_op | source)
XLA Modules:
  0.0 163.1 jit_solution(6345270226951938472)
XLA Ops:
  0.7 30.7 %all-gather = bf16[2048,128]{1,0:T(8,128)(2,1)S(1)} all-gather(bf16[512,128]{1,0:T(8,128)(2,1)} %param.4), channel_id=2, replica_groups={{0,4,8,12},{1,5,9,13},{2,6,10,14},{3,7,11,15},{16,20,24,28},{17,21,25,2..., dimensions={0}, use_global_device_ids=true | all-gather | bytes 655360 | tf_op jit(solution)/shard_map/all_gather | solution.py:151
  31.4 3.3 %collective-permute-start.1 = (bf16[4,512,128]{2,1,0:T(8,128)(2,1)S(1)}, bf16[4,512,128]{2,1,0:T(8,128)(2,1)S(1)}, u32[]{:S(2)}, u32[]{:S(2)}) collective-permute-start(bf16[4,512,128]{2,1,0:T(8,128)(2,1)S(1)} %bitcast.36), channel_id=1, source_target_pairs={{1,0},{2,1},{3,2},{4,3},{5,4},{6,5},{7,6},{8,7},{9,8},{10,9},{11,1... | collective-permute-start | bytes 1572872 | tf_op jit(solution)/shard_map/ppermute | solution.py:13
  34.6 2.0 %collective-permute-start.4 = (bf16[4,512,128]{2,1,0:T(8,128)(2,1)S(1)}, bf16[4,512,128]{2,1,0:T(8,128)(2,1)S(1)}, u32[]{:S(2)}, u32[]{:S(2)}) collective-permute-start(bf16[4,512,128]{2,1,0:T(8,128)(2,1)S(1)} %bitcast.37), channel_id=1, source_target_pairs={{15,0},{0,1},{1,2},{2,3},{3,4},{4,5},{5,6},{6,7},{7,8},{8,9},{9,10... | collective-permute-start | bytes 1572872 | tf_op jit(solution)/shard_map/ppermute | solution.py:13
  36.6 0.7 fusion.17
  37.4 3.6 %collective-permute-start.2 = (bf16[2,512,128]{2,1,0:T(8,128)(2,1)S(1)}, bf16[2,512,128]{2,1,0:T(8,128)(2,1)}, u32[]{:S(2)}, u32[]{:S(2)}) collective-permute-start(bf16[2,512,128]{2,1,0:T(8,128)(2,1)S(1)} %bitcast.43), channel_id=1, source_target_pairs={{2,0},{3,1},{4,2},{5,3},{6,4},{7,5},{8,6},{9,7},{10,8},{11,9},{12,... | collective-permute-start | bytes 786440 | tf_op jit(solution)/shard_map/ppermute | solution.py:13
  41.0 2.6 %collective-permute-start.3 = (bf16[2,512,128]{2,1,0:T(8,128)(2,1)}, bf16[2,512,128]{2,1,0:T(8,128)(2,1)}, u32[]{:S(2)}, u32[]{:S(2)}) collective-permute-start(bf16[2,512,128]{2,1,0:T(8,128)(2,1)} %bitcast.7), channel_id=1, source_target_pairs={{14,0},{15,1},{0,2},{1,3},{2,4},{3,5},{4,6},{5,7},{6,8},{7,9},{8,1... | collective-permute-start | bytes 786440 | tf_op jit(solution)/shard_map/ppermute | solution.py:13
  43.7 1.1 broadcast_in_dim.2
  44.8 4.2 %all-to-all-start.2 = ((bf16[4,224,512]{2,1,0:T(8,128)(2,1)}), bf16[4,224,512]{2,1,0:T(8,128)(2,1)S(1)}, u32[]{:S(2)}, u32[]{:S(2)}) async-start(bf16[4,224,512]{2,1,0:T(8,128)(2,1)} %broadcast_in_dim.2), calls=%async_computation.2 | async-start | bytes 1835008 | tf_op jit(solution)/shard_map/all_to_all | solution.py:144
  49.0 7.1 %reshape.10 = bf16[224,4,2,1024]{3,2,1,0:T(2,128)(2,1)} reshape(bf16[224,8192]{1,0:T(8,128)(2,1)} %param.7) | data formatting | bytes 7340032 | tf_op jit(solution)/shard_map/reshape | solution.py:147
  56.1 8.3 %constant_dynamic-slice_fusion = bf16[224,4,1,1024]{3,2,1,0:T(2,128)(2,1)} fusion(bf16[224,4,2,1024]{3,2,1,0:T(2,128)(2,1)} %reshape.10, s32[]{:T(128)S(6)} %select_n.24), kind=kLoop, calls=%fused_computation.29 | loop fusion | bytes 3670020 | tf_op jit(solution)/shard_map/jit(dynamic_index_in_dim)/dynamic_slice | solution.py:147
  64.5 5.3 %copy.10 = bf16[224,4,1,1024]{3,0,1,2:T(8,128)(2,1)} copy(bf16[224,4,1,1024]{3,2,1,0:T(2,128)(2,1)} %constant_dynamic-slice_fusion) | data formatting | bytes 3670016
  69.8 1.0 constant_dynamic-update-slice_fusion.1
  70.8 1.0 constant_dynamic-update-slice_fusion.a2.b2.s2
  71.8 0.9 copy-done.1
  72.7 4.4 %all-to-all-start = ((bf16[4,224,1024]{2,1,0:T(8,128)(2,1)}), bf16[4,224,1024]{2,1,0:T(8,128)(2,1)}, u32[]{:S(2)}, u32[]{:S(2)}) async-start(bf16[4,224,1024]{2,1,0:T(8,128)(2,1)} %bitcast.42), calls=%async_computation | async-start | bytes 3670016 | tf_op jit(solution)/shard_map/all_to_all | solution.py:148
  77.1 1.5 fusion.hid
  78.6 2.9 %shard_map.68 = bf16[4,224,1024]{2,1,0:T(8,128)(2,1)} custom-call(s32[3]{0:T(128)S(1)} %pad_add_fusion.pos, bf16[4,224,512]{2,1,0:T(8,128)(2,1)S(1)} %fusion.hid, bf16[4,512,128]{2,1,0:T(8,128)(2,1)S(1)} %bitcast.38, bf16[4,512,128]{2,1,0:T(8,128)(2,1)S(1)} %collective-permute-done.1.a1.b1.s1, ...), custom_call_target="tpu_custom_call" | custom-call | flops 939524096 | bytes 4194304 | tf_op jit(solution)/shard_map/pallas_call | solution.py:47
  81.5 7.6 %collective-permute-start.5 = (bf16[4,224,1024]{2,1,0:T(8,128)(2,1)}, bf16[4,224,1024]{2,1,0:T(8,128)(2,1)}, u32[]{:S(2)}, u32[]{:S(2)}) collective-permute-start(bf16[4,224,1024]{2,1,0:T(8,128)(2,1)} %shard_map.68), channel_id=1, source_target_pairs={{0,64},{64,0},{128,192},{192,128},{256,320},{320,256},{384,448},{4... | collective-permute-start | bytes 5505032 | tf_op jit(solution)/shard_map/ppermute | solution.py:17
  89.1 4.2 %all-to-all-done.wa = bf16[4,224,1024]{2,1,0:T(8,128)(2,1)} async-done(((bf16[4,224,1024]{2,1,0:T(8,128)(2,1)}), bf16[4,224,1024]{2,1,0:T(8,128)(2,1)}, u32[]{:S(2)}, u32[]{:S(2)}) %all-to-all-start) | async-done | bytes 1835040 | tf_op jit(solution)/shard_map/all_to_all | solution.py:148
  93.3 8.5 %collective-permute-start = (bf16[4,224,1024]{2,1,0:T(8,128)(2,1)}, bf16[4,224,1024]{2,1,0:T(8,128)(2,1)}, u32[]{:S(2)}, u32[]{:S(2)}) collective-permute-start(bf16[4,224,1024]{2,1,0:T(8,128)(2,1)} %all-to-all-done.wa), channel_id=1, source_target_pairs={{0,64},{64,0},{128,192},{192,128},{256,320},{320,256},{384,448},{4... | collective-permute-start | bytes 5505032 | tf_op jit(solution)/shard_map/ppermute | solution.py:17
  101.8 3.2 %shard_map.69 = bf16[4,224,1024]{2,1,0:T(8,128)(2,1)S(1)} custom-call(s32[3]{0:T(128)S(1)} %pad_add_fusion.pos, bf16[4,224,512]{2,1,0:T(8,128)(2,1)S(1)} %fusion.hid, bf16[4,512,128]{2,1,0:T(8,128)(2,1)S(1)} %bitcast.39, bf16[4,512,128]{2,1,0:T(8,128)(2,1)S(1)} %collective-permute-done.1.a1.b1.s1, ...), custom_call_target="tpu_custom_call" | custom-call | flops 939524096 | bytes 4194304 | tf_op jit(solution)/shard_map/pallas_call | solution.py:47
  105.0 1.2 copy-done
  106.3 4.4 %all-to-all-start.3 = ((bf16[4,224,1024]{2,1,0:T(8,128)(2,1)}), bf16[4,224,1024]{2,1,0:T(8,128)(2,1)}, u32[]{:S(2)}, u32[]{:S(2)}) async-start(bf16[4,224,1024]{2,1,0:T(8,128)(2,1)} %copy-done), calls=%async_computation.3 | async-start | bytes 3670016 | tf_op jit(solution)/shard_map/all_to_all | solution.py:159
  110.7 6.0 %shard_map.67 = bf16[4,224,512]{2,1,0:T(8,128)(2,1)} custom-call(s32[3]{0:T(128)S(1)} %pad_add_fusion.pos, bf16[4,224,1024]{2,1,0:T(8,128)(2,1)} %all-to-all-done.wa, bf16[4,224,1024]{2,1,0:T(8,128)(2,1)} %collective-permute-done.wb, bf16[4,512,128]{2,1,0:T(8,128)(2,1)S(1)} %bitcast.40, bf16[4,512,128]{2,1,0:T(8,128)(2,1)S(1)} %collective-permute-done.1.a1.b1.s1, ...), custom_call_target="tpu_custom_call" | custom-call | flops 1879048192 | bytes 7340032 | tf_op jit(solution)/shard_map/pallas_call | solution.py:88
  116.7 17.5 %all-to-all-done.3.q = bf16[4,224,1024]{2,1,0:T(8,128)(2,1)} async-done(((bf16[4,224,1024]{2,1,0:T(8,128)(2,1)}), bf16[4,224,1024]{2,1,0:T(8,128)(2,1)}, u32[]{:S(2)}, u32[]{:S(2)}) %all-to-all-start.3) | async-done | bytes 1835040 | tf_op jit(solution)/shard_map/all_to_all | solution.py:159
  134.3 5.2 %all-to-all-start.1 = ((bf16[4,224,512]{2,1,0:T(8,128)(2,1)}), bf16[4,224,512]{2,1,0:T(8,128)(2,1)S(1)}, u32[]{:S(2)}, u32[]{:S(2)}) async-start(bf16[4,224,512]{2,1,0:T(8,128)(2,1)} %shard_map.67), calls=%async_computation.1 | async-start | bytes 1835008 | tf_op jit(solution)/shard_map/all_to_all | solution.py:168
  139.5 2.3 %shard_map.70 = bf16[224,1024]{1,0:T(8,128)(2,1)S(1)} custom-call(s32[3]{0:T(128)S(1)} %pad_add_fusion.pos, bf16[4,224,1024]{2,1,0:T(8,128)(2,1)} %all-to-all-done.3.q), custom_call_target="tpu_custom_call" | custom-call | flops 917504 | bytes 2293760 | tf_op jit(solution)/shard_map/pallas_call | solution.py:117
  141.8 3.7 %collective-permute-start.6 = (bf16[224,1024]{1,0:T(8,128)(2,1)S(1)}, bf16[224,1024]{1,0:T(8,128)(2,1)S(1)}, u32[]{:S(2)}, u32[]{:S(2)}) collective-permute-start(bf16[224,1024]{1,0:T(8,128)(2,1)S(1)} %shard_map.70), channel_id=1, source_target_pairs={{0,0},{16,176},{32,288},{48,400},{64,64},{80,240},{96,352},{112,46... | collective-permute-start | bytes 1376264 | tf_op jit(solution)/shard_map/ppermute | solution.py:166
  145.5 5.0 %all-to-all-done.1 = bf16[4,224,512]{2,1,0:T(8,128)(2,1)S(1)} async-done(((bf16[4,224,512]{2,1,0:T(8,128)(2,1)}), bf16[4,224,512]{2,1,0:T(8,128)(2,1)S(1)}, u32[]{:S(2)}, u32[]{:S(2)}) %all-to-all-start.1) | async-done | bytes 917536 | tf_op jit(solution)/shard_map/all_to_all | solution.py:168
  150.6 1.0 fusion.16
  151.6 10.7 %collective-permute-done.6 = bf16[224,1024]{1,0:T(8,128)(2,1)S(1)} collective-permute-done((bf16[224,1024]{1,0:T(8,128)(2,1)S(1)}, bf16[224,1024]{1,0:T(8,128)(2,1)S(1)}, u32[]{:S(2)}, u32[]{:S(2)}) %collective-permute-start.6) | collective-permute-done | bytes 458784 | tf_op jit(solution)/shard_map/ppermute | solution.py:166
  162.3 0.8 copy.13
  (16 shorter events, 0.4 us)
Async XLA Ops:
  0.6 42.9 %copy-start.2 = (bf16[512,224]{0,1:T(8,128)(2,1)S(1)}, bf16[512,224]{0,1:T(8,128)(2,1)}, u32[]{:S(2)}) copy-start(bf16[512,224]{0,1:T(8,128)(2,1)} %param.5) | copy-start | bytes 688132
  0.6 42.9 %copy-start.3 = (bf16[512,224]{0,1:T(8,128)(2,1)S(1)}, bf16[512,224]{0,1:T(8,128)(2,1)}, u32[]{:S(2)}) copy-start(bf16[512,224]{0,1:T(8,128)(2,1)} %param.6) | copy-start | bytes 688132
  31.4 47.2 %collective-permute-start.1 = (bf16[4,512,128]{2,1,0:T(8,128)(2,1)S(1)}, bf16[4,512,128]{2,1,0:T(8,128)(2,1)S(1)}, u32[]{:S(2)}, u32[]{:S(2)}) collective-permute-start(bf16[4,512,128]{2,1,0:T(8,128)(2,1)S(1)} %bitcast.36), channel_id=1, source_target_pairs={{1,0},{2,1},{3,2},{4,3},{5,4},{6,5},{7,6},{8,7},{9,8},{10,9},{11,1... | collective-permute-start | bytes 1572872 | tf_op jit(solution)/shard_map/ppermute | solution.py:13
  34.6 44.0 %collective-permute-start.4 = (bf16[4,512,128]{2,1,0:T(8,128)(2,1)S(1)}, bf16[4,512,128]{2,1,0:T(8,128)(2,1)S(1)}, u32[]{:S(2)}, u32[]{:S(2)}) collective-permute-start(bf16[4,512,128]{2,1,0:T(8,128)(2,1)S(1)} %bitcast.37), channel_id=1, source_target_pairs={{15,0},{0,1},{1,2},{2,3},{3,4},{4,5},{5,6},{6,7},{7,8},{8,9},{9,10... | collective-permute-start | bytes 1572872 | tf_op jit(solution)/shard_map/ppermute | solution.py:13
  37.4 32.4 %collective-permute-start.2 = (bf16[2,512,128]{2,1,0:T(8,128)(2,1)S(1)}, bf16[2,512,128]{2,1,0:T(8,128)(2,1)}, u32[]{:S(2)}, u32[]{:S(2)}) collective-permute-start(bf16[2,512,128]{2,1,0:T(8,128)(2,1)S(1)} %bitcast.43), channel_id=1, source_target_pairs={{2,0},{3,1},{4,2},{5,3},{6,4},{7,5},{8,6},{9,7},{10,8},{11,9},{12,... | collective-permute-start | bytes 786440 | tf_op jit(solution)/shard_map/ppermute | solution.py:13
  41.0 29.8 %collective-permute-start.3 = (bf16[2,512,128]{2,1,0:T(8,128)(2,1)}, bf16[2,512,128]{2,1,0:T(8,128)(2,1)}, u32[]{:S(2)}, u32[]{:S(2)}) collective-permute-start(bf16[2,512,128]{2,1,0:T(8,128)(2,1)} %bitcast.7), channel_id=1, source_target_pairs={{14,0},{15,1},{0,2},{1,3},{2,4},{3,5},{4,6},{5,7},{6,8},{7,9},{8,1... | collective-permute-start | bytes 786440 | tf_op jit(solution)/shard_map/ppermute | solution.py:13
  44.8 27.0 %all-to-all-start.2 = ((bf16[4,224,512]{2,1,0:T(8,128)(2,1)}), bf16[4,224,512]{2,1,0:T(8,128)(2,1)S(1)}, u32[]{:S(2)}, u32[]{:S(2)}) async-start(bf16[4,224,512]{2,1,0:T(8,128)(2,1)} %broadcast_in_dim.2), calls=%async_computation.2 | async-start | bytes 1835008 | tf_op jit(solution)/shard_map/all_to_all | solution.py:144
  71.8 0.9 copy-start.1
  72.7 20.6 %all-to-all-start = ((bf16[4,224,1024]{2,1,0:T(8,128)(2,1)}), bf16[4,224,1024]{2,1,0:T(8,128)(2,1)}, u32[]{:S(2)}, u32[]{:S(2)}) async-start(bf16[4,224,1024]{2,1,0:T(8,128)(2,1)} %bitcast.42), calls=%async_computation | async-start | bytes 3670016 | tf_op jit(solution)/shard_map/all_to_all | solution.py:148
  81.5 20.3 %collective-permute-start.5 = (bf16[4,224,1024]{2,1,0:T(8,128)(2,1)}, bf16[4,224,1024]{2,1,0:T(8,128)(2,1)}, u32[]{:S(2)}, u32[]{:S(2)}) collective-permute-start(bf16[4,224,1024]{2,1,0:T(8,128)(2,1)} %shard_map.68), channel_id=1, source_target_pairs={{0,64},{64,0},{128,192},{192,128},{256,320},{320,256},{384,448},{4... | collective-permute-start | bytes 5505032 | tf_op jit(solution)/shard_map/ppermute | solution.py:17
  93.3 17.4 %collective-permute-start = (bf16[4,224,1024]{2,1,0:T(8,128)(2,1)}, bf16[4,224,1024]{2,1,0:T(8,128)(2,1)}, u32[]{:S(2)}, u32[]{:S(2)}) collective-permute-start(bf16[4,224,1024]{2,1,0:T(8,128)(2,1)} %all-to-all-done.wa), channel_id=1, source_target_pairs={{0,64},{64,0},{128,192},{192,128},{256,320},{320,256},{384,448},{4... | collective-permute-start | bytes 5505032 | tf_op jit(solution)/shard_map/ppermute | solution.py:17
  105.0 1.3 copy-start
  106.3 28.0 %all-to-all-start.3 = ((bf16[4,224,1024]{2,1,0:T(8,128)(2,1)}), bf16[4,224,1024]{2,1,0:T(8,128)(2,1)}, u32[]{:S(2)}, u32[]{:S(2)}) async-start(bf16[4,224,1024]{2,1,0:T(8,128)(2,1)} %copy-done), calls=%async_computation.3 | async-start | bytes 3670016 | tf_op jit(solution)/shard_map/all_to_all | solution.py:159
  134.3 16.2 %all-to-all-start.1 = ((bf16[4,224,512]{2,1,0:T(8,128)(2,1)}), bf16[4,224,512]{2,1,0:T(8,128)(2,1)S(1)}, u32[]{:S(2)}, u32[]{:S(2)}) async-start(bf16[4,224,512]{2,1,0:T(8,128)(2,1)} %shard_map.67), calls=%async_computation.1 | async-start | bytes 1835008 | tf_op jit(solution)/shard_map/all_to_all | solution.py:168
  141.8 20.4 %collective-permute-start.6 = (bf16[224,1024]{1,0:T(8,128)(2,1)S(1)}, bf16[224,1024]{1,0:T(8,128)(2,1)S(1)}, u32[]{:S(2)}, u32[]{:S(2)}) collective-permute-start(bf16[224,1024]{1,0:T(8,128)(2,1)S(1)} %shard_map.70), channel_id=1, source_target_pairs={{0,0},{16,176},{32,288},{48,400},{64,64},{80,240},{96,352},{112,46... | collective-permute-start | bytes 1376264 | tf_op jit(solution)/shard_map/ppermute | solution.py:166

commit v2 on v0

v2 whole, which is shorter than its diff:
```python
import jax
import jax.numpy as jnp
from jax import lax
from jax.experimental import pallas as pl
from jax.experimental.pallas import tpu as pltpu
from jax.sharding import PartitionSpec as P

ZG = [[g + 4 * j for j in range(4)] for g in range(4)]

def from_col(a, k):
    return lax.ppermute(a, "col", [((i + k) % 16, i) for i in range(16)])


def other_core(a):
    return lax.ppermute(a, "depth", [(i, i ^ 1) for i in range(8)])


def columns_kernel(pos, *refs):
    for i in range(4):
        refs[4][i] = refs[i][...]


def columns_call(pos, w):
    f, d = w.shape
    return pl.pallas_call(
        columns_kernel,
        grid_spec=pltpu.PrefetchScalarGridSpec(
            num_scalar_prefetch=1,
            grid=(1,),
            in_specs=[pl.BlockSpec((f, d // 8), lambda g, p, i=i: (0, 2 * i + p[0])) for i in range(4)],
            out_specs=pl.BlockSpec((4, f, d // 8), lambda g, p: (0, 0, 0)),
        ),
        out_shape=jax.ShapeDtypeStruct((4, f, d // 8), jnp.bfloat16),
        compiler_params=pltpu.CompilerParams(vmem_limit_bytes=32 * 1024 * 1024),
        cost_estimate=pl.CostEstimate(flops=0, bytes_accessed=2 * f * d, transcendentals=0),
    )(pos, w, w, w, w)


def hidden_kernel(gate, up, after, out):
    g = gate[...].astype(jnp.float32)
    out[...] = (g * jax.nn.sigmoid(g) * up[...].astype(jnp.float32)).astype(out.dtype)


def hidden_call(gate, up, after):
    spec = pl.BlockSpec(gate.shape, lambda i: (0, 0))
    return pl.pallas_call(
        hidden_kernel,
        grid=(1,),
        in_specs=[spec, spec, pl.BlockSpec(memory_space=pl.ANY)],
        out_specs=spec,
        out_shape=jax.ShapeDtypeStruct(gate.shape, jnp.bfloat16),
        cost_estimate=pl.CostEstimate(flops=0, bytes_accessed=6 * gate.size, transcendentals=gate.size),
    )(gate, up, after)


def set_blocks(sets, halves):
    specs, args = [], []
    for h in halves:
        for s in sets:
            for q in range(2):
                if isinstance(s, tuple):
                    specs.append(pl.BlockSpec((1, 512, 128), lambda i, p, h=h: (p[h], 0, 0)))
                    args.append(s[q])
                else:
                    specs.append(pl.BlockSpec((1, 512, 128), lambda i, p, h=h, q=q: (2 * p[h] + q, 0, 0)))
                    args.append(s)
    return specs, args


def gather_features(pos, blocks, cat):
    for k in range(cat.shape[0]):
        for r in range(4):
            for q in range(2):
                at = pl.multiple_of(q * 512 + lax.rem(pos[2] + r, 4) * 128, 128)
                cat[k, :, pl.ds(at, 128)] = blocks[8 * k + 2 * r + q][0]


def partial_kernel(pos, *refs):
    cat = refs[-1]
    gather_features(pos, refs[4:12], cat)
    h = jnp.concatenate([refs[j][0] for j in range(4)], axis=0)
    p = jnp.dot(h, cat[0], preferred_element_type=jnp.float32) * (1.0 / 64.0)
    f = refs[0].shape[1]
    if len(refs) == 14:
        for j in range(4):
            refs[12][j] = p[j * f : j * f + f].astype(jnp.bfloat16)
    else:
        got, outs = refs[12], refs[13:17]
        for j in range(4):
            outs[j][...] = (p[j * f : j * f + f] + got[j].astype(jnp.float32)).astype(jnp.bfloat16)


def partial_call(pos, which, hid, sets, got=None):
    n, f, t = hid.shape
    specs, args = set_blocks(sets, (which,))
    rows = [pl.BlockSpec((1, f, t), lambda i, p, j=j: (lax.rem(p[4] + 4 + j - p[3], 4), 0, 0)) for j in range(4)]
    whole = pl.BlockSpec((n, f, 1024), lambda i, p: (0, 0, 0))
    one = pl.BlockSpec((f, 1024), lambda i, p: (0, 0))
    if got is None:
        out_specs, out_shape = whole, jax.ShapeDtypeStruct((n, f, 1024), jnp.bfloat16)
    else:
        out_specs, out_shape = [one] * 4, [jax.ShapeDtypeStruct((f, 1024), jnp.bfloat16)] * 4
        specs, args = specs + [whole], args + [got]
    return pl.pallas_call(
        partial_kernel,
        grid_spec=pltpu.PrefetchScalarGridSpec(
            num_scalar_prefetch=1,
            grid=(1,),
            in_specs=rows + specs,
            out_specs=out_specs,
            scratch_shapes=[pltpu.VMEM((1, t, 1024), jnp.bfloat16)],
        ),
        out_shape=out_shape,
        compiler_params=pltpu.CompilerParams(vmem_limit_bytes=48 * 1024 * 1024),
        cost_estimate=pl.CostEstimate(flops=2 * n * f * t * 1024, bytes_accessed=5 * 1024 * 1024, transcendentals=0),
    )(pos, hid, hid, hid, hid, *args)


def sum_kernel(a, b, c, d, out):
    total = a[...].astype(jnp.float32) + b[...].astype(jnp.float32)
    out[...] = (total + c[...].astype(jnp.float32) + d[...].astype(jnp.float32)).astype(out.dtype)


def sum_call(parts):
    f, d = parts[0].shape
    spec = pl.BlockSpec((f // 2, d), lambda i: (i, 0))
    return pl.pallas_call(
        sum_kernel,
        grid=(2,),
        in_specs=[spec] * 4,
        out_specs=spec,
        out_shape=jax.ShapeDtypeStruct((f, d), jnp.bfloat16),
        cost_estimate=pl.CostEstimate(flops=3 * f * d, bytes_accessed=10 * f * d, transcendentals=0),
    )(*parts)


def hidden_grad_kernel(pos, wa, wb, *refs):
    blocks, out, cat = refs[:16], refs[16], refs[17]
    n, f, d = wa.shape

    @pl.when(pl.program_id(0) == 0)
    def _():
        gather_features(pos, blocks, cat)

    total = None
    for k, w in enumerate((wa, wb)):
        part = lax.dot_general(
            w[...].reshape(n * f, d), cat[k], (((1,), (1,)), ((), ())), preferred_element_type=jnp.float32
        )
        total = part if total is None else total + part
    out[...] = total.astype(out.dtype).reshape(out.shape)


def hidden_grad_call(pos, wa, wb, sets):
    n, f, d = wa.shape
    t = 512
    specs, args = set_blocks(sets, (0, 1))
    wspec = pl.BlockSpec((2, f, d), lambda i, p: (i, 0, 0))
    return pl.pallas_call(
        hidden_grad_kernel,
        grid_spec=pltpu.PrefetchScalarGridSpec(
            num_scalar_prefetch=1,
            grid=(2,),
            in_specs=[wspec, wspec] + specs,
            out_specs=pl.BlockSpec((2, f, t), lambda i, p: (i, 0, 0)),
            scratch_shapes=[pltpu.VMEM((2, t, d), jnp.bfloat16)],
        ),
        out_shape=jax.ShapeDtypeStruct((n, f, t), jnp.bfloat16),
        compiler_params=pltpu.CompilerParams(vmem_limit_bytes=48 * 1024 * 1024),
        cost_estimate=pl.CostEstimate(flops=4 * n * f * t * d, bytes_accessed=7 * 1024 * 1024, transcendentals=0),
    )(pos, wa, wb, *args)


def shards(grad_out, gate_pre, up_pre, down_weight):
    depth, row, col = lax.axis_index("depth"), lax.axis_index("row"), lax.axis_index("col")
    pos = jnp.stack([depth % 2, 1 - depth % 2, col % 4, row, depth // 2]).astype(jnp.int32)

    wa = lax.all_to_all(columns_call(pos, down_weight), "row", 0, 0)
    wb = other_core(wa)

    set0 = lax.all_gather(grad_out, "col", axis=0, axis_index_groups=ZG)
    set2 = (from_col(set0[0::2], 2), from_col(set0[1::2], -2))
    set1 = from_col(set0, 1)
    set3 = from_col(set0, -1)
    sets = (set0, set1, set2, set3)

    hid = lax.all_gather(hidden_call(gate_pre.T, up_pre.T, set0), "row", axis=0)

    away = partial_call(pos, 1, hid, sets)
    both = partial_call(pos, 0, hid, sets, other_core(away))
    parts = [both[0]]
    for j in (1, 3, 2):
        parts.append(lax.ppermute(both[j], "depth", [(i, (i + 2 * j) % 8) for i in range(8)]))
    perm = []
    for y in range(4):
        for c in range(2):
            for x in range(4):
                perm.append(((2 * y + c) * 4 + x, (2 * x + c) * 4 + (y - x) % 4))
    grad_down = lax.ppermute(sum_call(parts), ("depth", "row"), perm)

    gate = gate_pre.T.astype(jnp.float32)
    upval = up_pre.T.astype(jnp.float32)
    sigma = jax.nn.sigmoid(gate)
    active = gate * sigma
    terms = lax.all_to_all(hidden_grad_call(pos, wa, wb, sets), "row", 0, 0)
    grad_hidden = terms.astype(jnp.float32).sum(0)
    grad_up = (grad_hidden * active).astype(jnp.bfloat16)
    grad_gate = (grad_hidden * upval * sigma * (1.0 + gate * (1.0 - sigma))).astype(jnp.bfloat16)
    return (grad_gate.T, grad_up.T, grad_down)


def solution(mesh):
    in_specs = (
        P("depth", ("row", "col")),
        P("depth", ("row", "col")),
        P("depth", ("row", "col")),
        P(("row", "col"), None),
    )
    out_specs = (P("depth", ("row", "col")), P("depth", ("row", "col")), P(("row", "col"), "depth"))
    return jax.shard_map(shards, mesh=mesh, in_specs=in_specs, out_specs=out_specs, check_vma=False)
```

time: 237 us -> 139 us (0.59)
  waiting for transfers between devices: 204 us -> 17.4 us
  starting transfers between devices: 0.08 us -> 47.3 us
  blocking collectives: 0 us -> 43.6 us
  Pallas kernels: 0 us -> 19.1 us
  matrix products: 15.6 us -> 0 us
  between operations: 14.1 us -> 0.86 us
  local copies, waits for them, and re-layouts: 0.01 us -> 6.68 us
    all_gather x1 -> x0, waiting for transfers between devices: 164 us -> none  [shards(): piece = lax.all_gather(grad_out, ('row', 'col'), axis=1, tiled=True)]
    all_gather x0 -> x2, blocking collectives: none -> 43.6 us  [the longest x1 31 us: shards(): set0 = lax.all_gather(grad_out, 'col', axis=0, axis_index_groups=ZG)]
    reduce_scatter x1 -> x0, waiting for transfers between devices: 39.4 us -> none  [shards(): lax.psum_scatter((weight_term * scale).astype(jnp.bfloat16), 'depth', sca...]
    ppermute x0 -> x10, starting transfers between devices: none -> 38.7 us  [the longest x2 11.5 us: other_core(): return lax.ppermute(a, 'depth', [(i, i ^ 1) for i in range(8)])]
    pallas_call x0 -> x6, Pallas kernels: none -> 19.1 us  [the longest x2 7.19 us: partial_call(): pl.pallas_call(partial_kernel, grid_spec=pltpu.PrefetchScalarGridSpec(num...]
    ppermute x0 -> x10, waiting for transfers between devices: none -> 17.4 us  [the longest x1 10.5 us: shards(): grad_down = lax.ppermute(sum_call(parts), ('depth', 'row'), perm)]
    dot_general x2 -> x0, matrix products: 15.6 us -> none  [the longest x1 7.99 us: shards(): lax.dot_general(piece, down_weight, (((1,), (1,)), ((), ())), preferred_e...]
    all_to_all x0 -> x2, starting transfers between devices: none -> 8.56 us  [the longest x1 4.51 us: shards(): wa = lax.all_to_all(columns_call(pos, down_weight), 'row', 0, 0)]
  transfers between devices with their start and end apart: 2 -> 12, of which waited for: 2 -> 3; matrix products, arithmetic and copies ran while one was open for 3% -> 1% of each run, Pallas kernels for 0% -> 13%
where the time goes in v2:
time: 139 us; the launch traced here: 136 us
  starting transfers between devices  47.3 us (34%)
  blocking collectives  43.6 us (31%)
  Pallas kernels  19.1 us (14%)
  waiting for transfers between devices  17.4 us (13%)
  local copies, waits for them, and re-layouts  6.68 us (5%)
    all_gather x1, blocking collectives, shards(): set0 = lax.all_gather(grad_out, 'col', axis=0, axis_index_groups=ZG)  31 us
    all_gather x1, blocking collectives, shards(): hid = lax.all_gather(hidden_call(gate_pre.T, up_pre.T, set0), 'row', axis=0)  12.6 us
    ppermute x2, starting transfers between devices, other_core(): return lax.ppermute(a, 'depth', [(i, i ^ 1) for i in range(8)])  11.5 us
    ppermute x4, starting transfers between devices, from_col(): return lax.ppermute(a, 'col', [((i + k) % 16, i) for i in range(16)])  11.5 us
    ppermute x1, waiting for transfers between devices, shards(): grad_down = lax.ppermute(sum_call(parts), ('depth', 'row'), perm)  10.5 us
    ppermute x3, starting transfers between devices, shards(): lax.ppermute(both[j], 'depth', [(i, (i + 2 * j) % 8) for i in range(8)])  10.1 us
    pallas_call x2, Pallas kernels, partial_call(): pl.pallas_call(partial_kernel, grid_spec=pltpu.PrefetchScalarGridSpec(num...  7.19 us
    unnamed x23, local copies, waits for them, and re-layouts  5.86 us
  transfers between devices with their start and end apart: 12, of which 3 were waited for; matrix products, arithmetic and copies ran while one was open for 1% of the time, Pallas kernels for 13%

profile of v2, /device:TPU:7, one launch (start us, length us, event | category | flops | bytes accessed | tf_op | source)
XLA Modules:
  0.0 136.1 jit_solution(6060535861504532653)
XLA Ops:
  0.7 0.1 stack.23.pos
  0.7 2.0 %copy-done.3 = bf16[224,8192]{1,0:T(8,128)(2,1)S(1)} copy-done((bf16[224,8192]{1,0:T(8,128)(2,1)S(1)}, bf16[224,8192]{1,0:T(8,128)(2,1)}, u32[]{:S(2)}) %copy-start.3) | copy-done | bytes 3670040
  2.8 1.9 %shard_map.67 = bf16[4,224,1024]{2,1,0:T(8,128)(2,1)} custom-call(s32[5]{0:T(128)S(1)} %stack.23.pos, bf16[224,8192]{1,0:T(8,128)(2,1)S(1)} %copy-done.3, bf16[224,8192]{1,0:T(8,128)(2,1)S(1)} %copy-done.3, bf16[224,8192]{1,0:T(8,128)(2,1)S(1)} %copy-done.3, bf16[224,8192]{1,0:T(8,128)(2,1)S(1)} %copy-done.3), custom_call_target="tpu_custom_call" | custom-call | bytes 3670016 | tf_op jit(solution)/shard_map/pallas_call | solution.py:25
  4.7 4.5 %all-to-all-start = ((bf16[4,224,1024]{2,1,0:T(8,128)(2,1)}), bf16[4,224,1024]{2,1,0:T(8,128)(2,1)}, u32[]{:S(2)}, u32[]{:S(2)}) async-start(bf16[4,224,1024]{2,1,0:T(8,128)(2,1)} %shard_map.67), calls=%async_computation | async-start | bytes 3670016 | tf_op jit(solution)/shard_map/all_to_all | solution.py:178
  9.2 31.0 %all-gather = bf16[2048,128]{1,0:T(8,128)(2,1)S(1)} all-gather(bf16[512,128]{1,0:T(8,128)(2,1)S(1)} %copy-done.10), channel_id=2, replica_groups={{0,4,8,12},{1,5,9,13},{2,6,10,14},{3,7,11,15},{16,20,24,28},{17,21,25,2..., dimensions={0}, use_global_device_ids=true | all-gather | bytes 655360 | tf_op jit(solution)/shard_map/all_gather | solution.py:181
  40.2 3.4 %collective-permute-start.1 = (bf16[4,512,128]{2,1,0:T(8,128)(2,1)S(1)}, bf16[4,512,128]{2,1,0:T(8,128)(2,1)S(1)}, u32[]{:S(2)}, u32[]{:S(2)}) collective-permute-start(bf16[4,512,128]{2,1,0:T(8,128)(2,1)S(1)} %bitcast.24), channel_id=1, source_target_pairs={{1,0},{2,1},{3,2},{4,3},{5,4},{6,5},{7,6},{8,7},{9,8},{10,9},{11,1... | collective-permute-start | bytes 1572872 | tf_op jit(solution)/shard_map/ppermute | solution.py:11
  43.6 1.9 %collective-permute-start.4 = (bf16[4,512,128]{2,1,0:T(8,128)(2,1)S(1)}, bf16[4,512,128]{2,1,0:T(8,128)(2,1)S(1)}, u32[]{:S(2)}, u32[]{:S(2)}) collective-permute-start(bf16[4,512,128]{2,1,0:T(8,128)(2,1)S(1)} %bitcast.25), channel_id=1, source_target_pairs={{15,0},{0,1},{1,2},{2,3},{3,4},{4,5},{5,6},{6,7},{7,8},{8,9},{9,10... | collective-permute-start | bytes 1572872 | tf_op jit(solution)/shard_map/ppermute | solution.py:11
  45.5 0.7 fusion.9
  46.2 3.3 %collective-permute-start.2 = (bf16[2,512,128]{2,1,0:T(8,128)(2,1)}, bf16[2,512,128]{2,1,0:T(8,128)(2,1)S(1)}, u32[]{:S(2)}, u32[]{:S(2)}) collective-permute-start(bf16[2,512,128]{2,1,0:T(8,128)(2,1)} %get-tuple-element.14), channel_id=1, source_target_pairs={{2,0},{3,1},{4,2},{5,3},{6,4},{7,5},{8,6},{9,7},{10,8},{11,9},{12,... | collective-permute-start | bytes 786440 | tf_op jit(solution)/shard_map/ppermute | solution.py:11
  49.6 2.8 %collective-permute-start.3 = (bf16[2,512,128]{2,1,0:T(8,128)(2,1)S(1)}, bf16[2,512,128]{2,1,0:T(8,128)(2,1)S(1)}, u32[]{:S(2)}, u32[]{:S(2)}) collective-permute-start(bf16[2,512,128]{2,1,0:T(8,128)(2,1)S(1)} %get-tuple-element.13), channel_id=1, source_target_pairs={{14,0},{15,1},{0,2},{1,3},{2,4},{3,5},{4,6},{5,7},{6,8},{7,9},{8,1... | collective-permute-start | bytes 786440 | tf_op jit(solution)/shard_map/ppermute | solution.py:11
  52.4 1.8 %shard_map.69 = bf16[224,512]{1,0:T(8,128)(2,1)} custom-call(bf16[224,512]{1,0:T(8,128)(2,1)} %bitcast.36, bf16[224,512]{1,0:T(8,128)(2,1)} %bitcast.37, bf16[4,512,128]{2,1,0:T(8,128)(2,1)} %bitcast.27), custom_call_target="tpu_custom_call" | custom-call | bytes 688128 | tf_op jit(solution)/shard_map/pallas_call | solution.py:46
  54.3 12.6 %all-gather.1 = bf16[896,512]{1,0:T(8,128)(2,1)S(1)} all-gather(bf16[224,512]{1,0:T(8,128)(2,1)} %shard_map.69), channel_id=3, replica_groups=mesh['depth'=8,'row'=4,'col'=16] {'row'}, dimensions={0}, use_global_device_ids=true | all-gather | bytes 1146880 | tf_op jit(solution)/shard_map/all_gather | solution.py:187
  66.9 1.0 copy-done.1
  68.0 3.1 %shard_map.70 = bf16[4,224,1024]{2,1,0:T(8,128)(2,1)} custom-call(s32[5]{0:T(128)S(1)} %stack.23.pos, bf16[4,224,512]{2,1,0:T(8,128)(2,1)S(1)} %bitcast.16, bf16[4,224,512]{2,1,0:T(8,128)(2,1)S(1)} %bitcast.17, bf16[4,224,512]{2,1,0:T(8,128)(2,1)S(1)} %bitcast.18, bf16[4,224,512]{2,1,0:T(8,128)(2,1)S(1)} %bitcast.19, bf16[4,512,128]{2,1,0:T(8,128)(2,1)S(1)} %bitcast.28, ...), custom_call_target="tpu_custom_call" | custom-call | flops 939524096 | bytes 5242880 | tf_op jit(solution)/shard_map/pallas_call | solution.py:104
  71.0 9.6 %collective-permute-start.5 = (bf16[4,224,1024]{2,1,0:T(8,128)(2,1)}, bf16[4,224,1024]{2,1,0:T(8,128)(2,1)}, u32[]{:S(2)}, u32[]{:S(2)}) collective-permute-start(bf16[4,224,1024]{2,1,0:T(8,128)(2,1)} %shard_map.70), channel_id=1, source_target_pairs={{0,64},{64,0},{128,192},{192,128},{256,320},{320,256},{384,448},{4... | collective-permute-start | bytes 5505032 | tf_op jit(solution)/shard_map/ppermute | solution.py:15
  80.7 1.9 %collective-permute-start = (bf16[4,224,1024]{2,1,0:T(8,128)(2,1)}, bf16[4,224,1024]{2,1,0:T(8,128)(2,1)S(1)}, u32[]{:S(2)}, u32[]{:S(2)}) collective-permute-start(bf16[4,224,1024]{2,1,0:T(8,128)(2,1)} %all-to-all-done.wa), channel_id=1, source_target_pairs={{0,64},{64,0},{128,192},{192,128},{256,320},{320,256},{384,448},{4... | collective-permute-start | bytes 5505032 | tf_op jit(solution)/shard_map/ppermute | solution.py:15
  82.6 1.8 %collective-permute-done.5.refs_12_ = bf16[4,224,1024]{2,1,0:T(8,128)(2,1)} collective-permute-done((bf16[4,224,1024]{2,1,0:T(8,128)(2,1)}, bf16[4,224,1024]{2,1,0:T(8,128)(2,1)}, u32[]{:S(2)}, u32[]{:S(2)}) %collective-permute-start.5) | collective-permute-done | bytes 1835040 | tf_op jit(solution)/shard_map/ppermute | solution.py:15
  84.4 4.1 %shard_map.71 = (bf16[224,1024]{1,0:T(8,128)(2,1)S(1)}, bf16[224,1024]{1,0:T(8,128)(2,1)}, bf16[224,1024]{1,0:T(8,128)(2,1)S(1)}, bf16[224,1024]{1,0:T(8,128)(2,1)}) custom-call(s32[5]{0:T(128)S(1)} %stack.23.pos, bf16[4,224,512]{2,1,0:T(8,128)(2,1)S(1)} %bitcast.20, bf16[4,224,512]{2,1,0:T(8,128)(2,1)S(1)} %bitcast.21, bf16[4,224,512]{2,1,0:T(8,128)(2,1)S(1)} %bitcast.22, ...), custom_call_target="tpu_custom_call" | custom-call | flops 939524096 | bytes 5242880 | tf_op jit(solution)/shard_map/pallas_call | solution.py:104
  88.5 0.8 copy-done.4
  89.3 3.2 %collective-permute-start.6 = (bf16[224,1024]{1,0:T(8,128)(2,1)}, bf16[224,1024]{1,0:T(8,128)(2,1)S(1)}, u32[]{:S(2)}, u32[]{:S(2)}) collective-permute-start(bf16[224,1024]{1,0:T(8,128)(2,1)} %get-tuple-element.8), channel_id=1, source_target_pairs={{0,128},{64,192},{128,256},{192,320},{256,384},{320,448},{384,0},{... | collective-permute-start | bytes 1376264 | tf_op jit(solution)/shard_map/ppermute | solution.py:193
  92.5 3.4 %collective-permute-start.7 = (bf16[224,1024]{1,0:T(8,128)(2,1)}, bf16[224,1024]{1,0:T(8,128)(2,1)S(1)}, u32[]{:S(2)}, u32[]{:S(2)}) collective-permute-start(bf16[224,1024]{1,0:T(8,128)(2,1)} %get-tuple-element.9), channel_id=1, source_target_pairs={{0,384},{64,448},{128,0},{192,64},{256,128},{320,192},{384,256},{4... | collective-permute-start | bytes 1376264 | tf_op jit(solution)/shard_map/ppermute | solution.py:193
  95.8 3.5 %collective-permute-start.8 = (bf16[224,1024]{1,0:T(8,128)(2,1)S(1)}, bf16[224,1024]{1,0:T(8,128)(2,1)}, u32[]{:S(2)}, u32[]{:S(2)}) collective-permute-start(bf16[224,1024]{1,0:T(8,128)(2,1)S(1)} %get-tuple-element.10), channel_id=1, source_target_pairs={{0,256},{64,320},{128,384},{192,448},{256,0},{320,64},{384,128},{4... | collective-permute-start | bytes 1376264 | tf_op jit(solution)/shard_map/ppermute | solution.py:193
  99.4 1.2 copy-done.5
  100.6 5.7 %shard_map.68 = bf16[4,224,512]{2,1,0:T(8,128)(2,1)} custom-call(s32[5]{0:T(128)S(1)} %stack.23.pos, bf16[4,224,1024]{2,1,0:T(8,128)(2,1)} %all-to-all-done.wa, bf16[4,224,1024]{2,1,0:T(8,128)(2,1)} %copy-done.5, bf16[4,512,128]{2,1,0:T(8,128)(2,1)S(1)} %bitcast.32, bf16[4,512,128]{2,1,0:T(8,128)(2,1)S(1)} %bitcast.33, ...), custom_call_target="tpu_custom_call" | custom-call | flops 1879048192 | bytes 7340032 | tf_op jit(solution)/shard_map/pallas_call | solution.py:159
  106.4 4.1 %all-to-all-start.1 = ((bf16[4,224,512]{2,1,0:T(8,128)(2,1)}), bf16[4,224,512]{2,1,0:T(8,128)(2,1)S(1)}, u32[]{:S(2)}, u32[]{:S(2)}) async-start(bf16[4,224,512]{2,1,0:T(8,128)(2,1)} %shard_map.68), calls=%async_computation.1 | async-start | bytes 1835008 | tf_op jit(solution)/shard_map/all_to_all | solution.py:205
  110.4 5.0 %collective-permute-done.8.d = bf16[224,1024]{1,0:T(8,128)(2,1)} collective-permute-done((bf16[224,1024]{1,0:T(8,128)(2,1)S(1)}, bf16[224,1024]{1,0:T(8,128)(2,1)}, u32[]{:S(2)}, u32[]{:S(2)}) %collective-permute-start.8) | collective-permute-done | bytes 458784 | tf_op jit(solution)/shard_map/ppermute | solution.py:193
  115.5 2.4 %shard_map.72 = bf16[224,1024]{1,0:T(8,128)(2,1)} custom-call(bf16[224,1024]{1,0:T(8,128)(2,1)} %copy-done.4, bf16[224,1024]{1,0:T(8,128)(2,1)} %copy-done.8, bf16[224,1024]{1,0:T(8,128)(2,1)} %copy-done.9, bf16[224,1024]{1,0:T(8,128)(2,1)} %collective-permute-done.8.d), custom_call_target="tpu_custom_call" | custom-call | flops 688128 | bytes 2293760 | tf_op jit(solution)/shard_map/pallas_call | solution.py:127
  117.9 5.7 %collective-permute-start.9 = (bf16[224,1024]{1,0:T(8,128)(2,1)}, bf16[224,1024]{1,0:T(8,128)(2,1)S(1)}, u32[]{:S(2)}, u32[]{:S(2)}) collective-permute-start(bf16[224,1024]{1,0:T(8,128)(2,1)} %shard_map.72), channel_id=1, source_target_pairs={{0,0},{16,176},{32,288},{48,400},{64,64},{80,240},{96,352},{112,46... | collective-permute-start | bytes 1376264 | tf_op jit(solution)/shard_map/ppermute | solution.py:199
  123.6 10.5 %collective-permute-done.9 = bf16[224,1024]{1,0:T(8,128)(2,1)S(1)} collective-permute-done((bf16[224,1024]{1,0:T(8,128)(2,1)}, bf16[224,1024]{1,0:T(8,128)(2,1)S(1)}, u32[]{:S(2)}, u32[]{:S(2)}) %collective-permute-start.9) | collective-permute-done | bytes 458784 | tf_op jit(solution)/shard_map/ppermute | solution.py:199
  134.1 0.1 convert_reduce_fusion
  134.3 1.0 fusion.7
  135.3 0.8 copy.8
  (27 shorter events, 0.1 us)
Async XLA Ops:
  0.7 2.0 %copy-start.3 = (bf16[224,8192]{1,0:T(8,128)(2,1)S(1)}, bf16[224,8192]{1,0:T(8,128)(2,1)}, u32[]{:S(2)}) copy-start(bf16[224,8192]{1,0:T(8,128)(2,1)} %refs_3_.1) | copy-start | bytes 11010052
  4.7 4.5 %copy-start.10 = (bf16[512,128]{1,0:T(8,128)(2,1)S(1)}, bf16[512,128]{1,0:T(8,128)(2,1)}, u32[]{:S(2)}) copy-start(bf16[512,128]{1,0:T(8,128)(2,1)} %param.4) | copy-start | bytes 393220
  4.7 76.0 %all-to-all-start = ((bf16[4,224,1024]{2,1,0:T(8,128)(2,1)}), bf16[4,224,1024]{2,1,0:T(8,128)(2,1)}, u32[]{:S(2)}, u32[]{:S(2)}) async-start(bf16[4,224,1024]{2,1,0:T(8,128)(2,1)} %shard_map.67), calls=%async_computation | async-start | bytes 3670016 | tf_op jit(solution)/shard_map/all_to_all | solution.py:178
  40.2 12.2 %copy-start = (bf16[2048,128]{1,0:T(8,128)(2,1)}, bf16[2048,128]{1,0:T(8,128)(2,1)S(1)}, u32[]{:S(2)}) copy-start(bf16[2048,128]{1,0:T(8,128)(2,1)S(1)} %all-gather) | copy-start | bytes 1572868
  40.2 26.7 %collective-permute-start.1 = (bf16[4,512,128]{2,1,0:T(8,128)(2,1)S(1)}, bf16[4,512,128]{2,1,0:T(8,128)(2,1)S(1)}, u32[]{:S(2)}, u32[]{:S(2)}) collective-permute-start(bf16[4,512,128]{2,1,0:T(8,128)(2,1)S(1)} %bitcast.24), channel_id=1, source_target_pairs={{1,0},{2,1},{3,2},{4,3},{5,4},{6,5},{7,6},{8,7},{9,8},{10,9},{11,1... | collective-permute-start | bytes 1572872 | tf_op jit(solution)/shard_map/ppermute | solution.py:11
  43.6 23.3 %collective-permute-start.4 = (bf16[4,512,128]{2,1,0:T(8,128)(2,1)S(1)}, bf16[4,512,128]{2,1,0:T(8,128)(2,1)S(1)}, u32[]{:S(2)}, u32[]{:S(2)}) collective-permute-start(bf16[4,512,128]{2,1,0:T(8,128)(2,1)S(1)} %bitcast.25), channel_id=1, source_target_pairs={{15,0},{0,1},{1,2},{2,3},{3,4},{4,5},{5,6},{6,7},{7,8},{8,9},{9,10... | collective-permute-start | bytes 1572872 | tf_op jit(solution)/shard_map/ppermute | solution.py:11
  46.2 20.7 %collective-permute-start.2 = (bf16[2,512,128]{2,1,0:T(8,128)(2,1)}, bf16[2,512,128]{2,1,0:T(8,128)(2,1)S(1)}, u32[]{:S(2)}, u32[]{:S(2)}) collective-permute-start(bf16[2,512,128]{2,1,0:T(8,128)(2,1)} %get-tuple-element.14), channel_id=1, source_target_pairs={{2,0},{3,1},{4,2},{5,3},{6,4},{7,5},{8,6},{9,7},{10,8},{11,9},{12,... | collective-permute-start | bytes 786440 | tf_op jit(solution)/shard_map/ppermute | solution.py:11
  49.6 17.3 %collective-permute-start.3 = (bf16[2,512,128]{2,1,0:T(8,128)(2,1)S(1)}, bf16[2,512,128]{2,1,0:T(8,128)(2,1)S(1)}, u32[]{:S(2)}, u32[]{:S(2)}) collective-permute-start(bf16[2,512,128]{2,1,0:T(8,128)(2,1)S(1)} %get-tuple-element.13), channel_id=1, source_target_pairs={{14,0},{15,1},{0,2},{1,3},{2,4},{3,5},{4,6},{5,7},{6,8},{7,9},{8,1... | collective-permute-start | bytes 786440 | tf_op jit(solution)/shard_map/ppermute | solution.py:11
  66.9 1.0 copy-start.1
  68.0 16.4 %copy-start.2 = (bf16[2048,128]{1,0:T(8,128)(2,1)S(1)}, bf16[2048,128]{1,0:T(8,128)(2,1)}, u32[]{:S(2)}) copy-start(bf16[2048,128]{1,0:T(8,128)(2,1)} %copy-done) | copy-start | bytes 1572868
  71.0 13.3 %collective-permute-start.5 = (bf16[4,224,1024]{2,1,0:T(8,128)(2,1)}, bf16[4,224,1024]{2,1,0:T(8,128)(2,1)}, u32[]{:S(2)}, u32[]{:S(2)}) collective-permute-start(bf16[4,224,1024]{2,1,0:T(8,128)(2,1)} %shard_map.70), channel_id=1, source_target_pairs={{0,64},{64,0},{128,192},{192,128},{256,320},{320,256},{384,448},{4... | collective-permute-start | bytes 5505032 | tf_op jit(solution)/shard_map/ppermute | solution.py:15
  80.7 18.7 %collective-permute-start = (bf16[4,224,1024]{2,1,0:T(8,128)(2,1)}, bf16[4,224,1024]{2,1,0:T(8,128)(2,1)S(1)}, u32[]{:S(2)}, u32[]{:S(2)}) collective-permute-start(bf16[4,224,1024]{2,1,0:T(8,128)(2,1)} %all-to-all-done.wa), channel_id=1, source_target_pairs={{0,64},{64,0},{128,192},{192,128},{256,320},{320,256},{384,448},{4... | collective-permute-start | bytes 5505032 | tf_op jit(solution)/shard_map/ppermute | solution.py:15
  88.5 0.8 copy-start.4
  89.3 21.1 %collective-permute-start.6 = (bf16[224,1024]{1,0:T(8,128)(2,1)}, bf16[224,1024]{1,0:T(8,128)(2,1)S(1)}, u32[]{:S(2)}, u32[]{:S(2)}) collective-permute-start(bf16[224,1024]{1,0:T(8,128)(2,1)} %get-tuple-element.8), channel_id=1, source_target_pairs={{0,128},{64,192},{128,256},{192,320},{256,384},{320,448},{384,0},{... | collective-permute-start | bytes 1376264 | tf_op jit(solution)/shard_map/ppermute | solution.py:193
  92.5 18.0 %collective-permute-start.7 = (bf16[224,1024]{1,0:T(8,128)(2,1)}, bf16[224,1024]{1,0:T(8,128)(2,1)S(1)}, u32[]{:S(2)}, u32[]{:S(2)}) collective-permute-start(bf16[224,1024]{1,0:T(8,128)(2,1)} %get-tuple-element.9), channel_id=1, source_target_pairs={{0,384},{64,448},{128,0},{192,64},{256,128},{320,192},{384,256},{4... | collective-permute-start | bytes 1376264 | tf_op jit(solution)/shard_map/ppermute | solution.py:193
  95.8 19.6 %collective-permute-start.8 = (bf16[224,1024]{1,0:T(8,128)(2,1)S(1)}, bf16[224,1024]{1,0:T(8,128)(2,1)}, u32[]{:S(2)}, u32[]{:S(2)}) collective-permute-start(bf16[224,1024]{1,0:T(8,128)(2,1)S(1)} %get-tuple-element.10), channel_id=1, source_target_pairs={{0,256},{64,320},{128,384},{192,448},{256,0},{320,64},{384,128},{4... | collective-permute-start | bytes 1376264 | tf_op jit(solution)/shard_map/ppermute | solution.py:193
  99.4 1.2 copy-start.5
  106.4 27.8 %all-to-all-start.1 = ((bf16[4,224,512]{2,1,0:T(8,128)(2,1)}), bf16[4,224,512]{2,1,0:T(8,128)(2,1)S(1)}, u32[]{:S(2)}, u32[]{:S(2)}) async-start(bf16[4,224,512]{2,1,0:T(8,128)(2,1)} %shard_map.68), calls=%async_computation.1 | async-start | bytes 1835008 | tf_op jit(solution)/shard_map/all_to_all | solution.py:205
  110.4 5.1 %copy-start.8 = (bf16[224,1024]{1,0:T(8,128)(2,1)}, bf16[224,1024]{1,0:T(8,128)(2,1)S(1)}, u32[]{:S(2)}) copy-start(bf16[224,1024]{1,0:T(8,128)(2,1)S(1)} %collective-permute-done.6.b) | copy-start | bytes 1376260
  110.4 5.0 %copy-start.9 = (bf16[224,1024]{1,0:T(8,128)(2,1)}, bf16[224,1024]{1,0:T(8,128)(2,1)S(1)}, u32[]{:S(2)}) copy-start(bf16[224,1024]{1,0:T(8,128)(2,1)S(1)} %collective-permute-done.7.c) | copy-start | bytes 1376260
  115.5 18.8 %copy-start.6 = (bf16[512,224]{0,1:T(8,128)(2,1)S(1)}, bf16[512,224]{0,1:T(8,128)(2,1)}, u32[]{:S(2)}) copy-start(bf16[512,224]{0,1:T(8,128)(2,1)} %param.5) | copy-start | bytes 688132
  115.5 18.8 %copy-start.7 = (bf16[512,224]{0,1:T(8,128)(2,1)S(1)}, bf16[512,224]{0,1:T(8,128)(2,1)}, u32[]{:S(2)}) copy-start(bf16[512,224]{0,1:T(8,128)(2,1)} %param.6) | copy-start | bytes 688132
  117.9 16.2 %collective-permute-start.9 = (bf16[224,1024]{1,0:T(8,128)(2,1)}, bf16[224,1024]{1,0:T(8,128)(2,1)S(1)}, u32[]{:S(2)}, u32[]{:S(2)}) collective-permute-start(bf16[224,1024]{1,0:T(8,128)(2,1)} %shard_map.72), channel_id=1, source_target_pairs={{0,0},{16,176},{32,288},{48,400},{64,64},{80,240},{96,352},{112,46... | collective-permute-start | bytes 1376264 | tf_op jit(solution)/shard_map/ppermute | solution.py:199

commit v3 on v2

--- a/solution.py
+++ b/solution.py
@@ -15,9 +15,16 @@
     return lax.ppermute(a, "depth", [(i, i ^ 1) for i in range(8)])
 
 
-def columns_kernel(pos, *refs):
-    for i in range(4):
-        refs[4][i] = refs[i][...]
+def columns_kernel(pos, w, out, sems):
+    d = out.shape[2]
+    copies = [
+        pltpu.make_async_copy(w.at[:, pl.ds(pl.multiple_of((2 * i + pos[0]) * d, d), d)], out.at[i], sems.at[i])
+        for i in range(4)
+    ]
+    for c in copies:
+        c.start()
+    for c in copies:
+        c.wait()
 
 
 def columns_call(pos, w):
@@ -27,13 +34,14 @@
         grid_spec=pltpu.PrefetchScalarGridSpec(
             num_scalar_prefetch=1,
             grid=(1,),
-            in_specs=[pl.BlockSpec((f, d // 8), lambda g, p, i=i: (0, 2 * i + p[0])) for i in range(4)],
+            in_specs=[pl.BlockSpec(memory_space=pltpu.HBM)],
             out_specs=pl.BlockSpec((4, f, d // 8), lambda g, p: (0, 0, 0)),
+            scratch_shapes=[pltpu.SemaphoreType.DMA((4,))],
         ),
         out_shape=jax.ShapeDtypeStruct((4, f, d // 8), jnp.bfloat16),
-        compiler_params=pltpu.CompilerParams(vmem_limit_bytes=32 * 1024 * 1024),
+        compiler_params=pltpu.CompilerParams(vmem_limit_bytes=12 * 1024 * 1024),
         cost_estimate=pl.CostEstimate(flops=0, bytes_accessed=2 * f * d, transcendentals=0),
-    )(pos, w, w, w, w)
+    )(pos, w)
 
 
 def hidden_kernel(gate, up, after, out):
@@ -49,6 +57,7 @@
         in_specs=[spec, spec, pl.BlockSpec(memory_space=pl.ANY)],
         out_specs=spec,
         out_shape=jax.ShapeDtypeStruct(gate.shape, jnp.bfloat16),
+        compiler_params=pltpu.CompilerParams(vmem_limit_bytes=8 * 1024 * 1024),
         cost_estimate=pl.CostEstimate(flops=0, bytes_accessed=6 * gate.size, transcendentals=gate.size),
     )(gate, up, after)
 
@@ -95,11 +104,11 @@
     specs, args = set_blocks(sets, (which,))
     rows = [pl.BlockSpec((1, f, t), lambda i, p, j=j: (lax.rem(p[4] + 4 + j - p[3], 4), 0, 0)) for j in range(4)]
     whole = pl.BlockSpec((n, f, 1024), lambda i, p: (0, 0, 0))
-    one = pl.BlockSpec((f, 1024), lambda i, p: (0, 0))
+    kept = pl.BlockSpec(memory_space=pltpu.VMEM)
     if got is None:
-        out_specs, out_shape = whole, jax.ShapeDtypeStruct((n, f, 1024), jnp.bfloat16)
+        out_specs, out_shape = kept, pltpu.VMEM((n, f, 1024), jnp.bfloat16)
     else:
-        out_specs, out_shape = [one] * 4, [jax.ShapeDtypeStruct((f, 1024), jnp.bfloat16)] * 4
+        out_specs, out_shape = [kept] * 4, [pltpu.VMEM((f, 1024), jnp.bfloat16)] * 4
         specs, args = specs + [whole], args + [got]
     return pl.pallas_call(
         partial_kernel,
@@ -111,62 +120,57 @@
             scratch_shapes=[pltpu.VMEM((1, t, 1024), jnp.bfloat16)],
         ),
         out_shape=out_shape,
-        compiler_params=pltpu.CompilerParams(vmem_limit_bytes=48 * 1024 * 1024),
+        compiler_params=pltpu.CompilerParams(vmem_limit_bytes=18 * 1024 * 1024),
         cost_estimate=pl.CostEstimate(flops=2 * n * f * t * 1024, bytes_accessed=5 * 1024 * 1024, transcendentals=0),
     )(pos, hid, hid, hid, hid, *args)
 
 
-def sum_kernel(a, b, c, d, out):
+def sum_kernel(a, b, c, d, after, out):
     total = a[...].astype(jnp.float32) + b[...].astype(jnp.float32)
     out[...] = (total + c[...].astype(jnp.float32) + d[...].astype(jnp.float32)).astype(out.dtype)
 
 
-def sum_call(parts):
+def sum_call(parts, after):
     f, d = parts[0].shape
-    spec = pl.BlockSpec((f // 2, d), lambda i: (i, 0))
     return pl.pallas_call(
         sum_kernel,
-        grid=(2,),
-        in_specs=[spec] * 4,
-        out_specs=spec,
-        out_shape=jax.ShapeDtypeStruct((f, d), jnp.bfloat16),
+        in_specs=[pl.BlockSpec(memory_space=pltpu.VMEM)] * 4 + [pl.BlockSpec(memory_space=pl.ANY)],
+        out_specs=pl.BlockSpec(memory_space=pltpu.VMEM),
+        out_shape=pltpu.VMEM((f, d), jnp.bfloat16),
+        compiler_params=pltpu.CompilerParams(vmem_limit_bytes=8 * 1024 * 1024),
         cost_estimate=pl.CostEstimate(flops=3 * f * d, bytes_accessed=10 * f * d, transcendentals=0),
-    )(*parts)
+    )(*parts, after)
 
 
 def hidden_grad_kernel(pos, wa, wb, *refs):
-    blocks, out, cat = refs[:16], refs[16], refs[17]
-    n, f, d = wa.shape
-
-    @pl.when(pl.program_id(0) == 0)
-    def _():
-        gather_features(pos, blocks, cat)
-
+    blocks, outs, cat = refs[:16], refs[16:20], refs[20]
+    gather_features(pos, blocks, cat)
+    f = wa.shape[1]
     total = None
     for k, w in enumerate((wa, wb)):
-        part = lax.dot_general(
-            w[...].reshape(n * f, d), cat[k], (((1,), (1,)), ((), ())), preferred_element_type=jnp.float32
-        )
+        rows = jnp.concatenate([w[lax.rem(pos[3] + j, 4)] for j in range(4)], axis=0)
+        part = lax.dot_general(rows, cat[k], (((1,), (1,)), ((), ())), preferred_element_type=jnp.float32)
         total = part if total is None else total + part
-    out[...] = total.astype(out.dtype).reshape(out.shape)
+    for j in range(4):
+        outs[j][...] = total[j * f : j * f + f].astype(jnp.bfloat16)
 
 
 def hidden_grad_call(pos, wa, wb, sets):
     n, f, d = wa.shape
     t = 512
     specs, args = set_blocks(sets, (0, 1))
-    wspec = pl.BlockSpec((2, f, d), lambda i, p: (i, 0, 0))
+    wspec = pl.BlockSpec((n, f, d), lambda i, p: (0, 0, 0))
     return pl.pallas_call(
         hidden_grad_kernel,
         grid_spec=pltpu.PrefetchScalarGridSpec(
             num_scalar_prefetch=1,
-            grid=(2,),
+            grid=(1,),
             in_specs=[wspec, wspec] + specs,
-            out_specs=pl.BlockSpec((2, f, t), lambda i, p: (i, 0, 0)),
+            out_specs=[pl.BlockSpec(memory_space=pltpu.VMEM)] * n,
             scratch_shapes=[pltpu.VMEM((2, t, d), jnp.bfloat16)],
         ),
-        out_shape=jax.ShapeDtypeStruct((n, f, t), jnp.bfloat16),
-        compiler_params=pltpu.CompilerParams(vmem_limit_bytes=48 * 1024 * 1024),
+        out_shape=[pltpu.VMEM((f, t), jnp.bfloat16)] * n,
+        compiler_params=pltpu.CompilerParams(vmem_limit_bytes=24 * 1024 * 1024),
         cost_estimate=pl.CostEstimate(flops=4 * n * f * t * d, bytes_accessed=7 * 1024 * 1024, transcendentals=0),
     )(pos, wa, wb, *args)
 
@@ -188,6 +192,7 @@
 
     away = partial_call(pos, 1, hid, sets)
     both = partial_call(pos, 0, hid, sets, other_core(away))
+    terms = hidden_grad_call(pos, wa, wb, sets)
     parts = [both[0]]
     for j in (1, 3, 2):
         parts.append(lax.ppermute(both[j], "depth", [(i, (i + 2 * j) % 8) for i in range(8)]))
@@ -196,14 +201,16 @@
         for c in range(2):
             for x in range(4):
                 perm.append(((2 * y + c) * 4 + x, (2 * x + c) * 4 + (y - x) % 4))
-    grad_down = lax.ppermute(sum_call(parts), ("depth", "row"), perm)
+    grad_down = lax.ppermute(sum_call(parts, terms[0]), ("depth", "row"), perm)
 
     gate = gate_pre.T.astype(jnp.float32)
     upval = up_pre.T.astype(jnp.float32)
     sigma = jax.nn.sigmoid(gate)
     active = gate * sigma
-    terms = lax.all_to_all(hidden_grad_call(pos, wa, wb, sets), "row", 0, 0)
-    grad_hidden = terms.astype(jnp.float32).sum(0)
+    grad_hidden = terms[0].astype(jnp.float32)
+    for j in (1, 3, 2):
+        got = lax.ppermute(terms[j], "row", [(i, (i + j) % 4) for i in range(4)])
+        grad_hidden = grad_hidden + got.astype(jnp.float32)
     grad_up = (grad_hidden * active).astype(jnp.bfloat16)
     grad_gate = (grad_hidden * upval * sigma * (1.0 + gate * (1.0 - sigma))).astype(jnp.bfloat16)
     return (grad_gate.T, grad_up.T, grad_down)

time: 139 us -> 130 us (0.935)
  the two profiles are of different devices: /device:TPU:7 before, /device:TPU:4 now
where the time goes in v3:
time: 130 us; the launch traced here: 129 us
  starting transfers between devices  55 us (42%)
  blocking collectives  42.3 us (33%)
  waiting for transfers between devices  14 us (11%)
  Pallas kernels  13 us (10%)
  local copies, waits for them, and re-layouts  2.95 us (2%)
    all_gather x1, blocking collectives, shards(): set0 = lax.all_gather(grad_out, 'col', axis=0, axis_index_groups=ZG)  29.1 us
    all_gather x1, blocking collectives, shards(): hid = lax.all_gather(hidden_call(gate_pre.T, up_pre.T, set0), 'row', axis=0)  13.2 us
    ppermute x4, starting transfers between devices, from_col(): return lax.ppermute(a, 'col', [((i + k) % 16, i) for i in range(16)])  12.6 us
    ppermute x3, starting transfers between devices, shards(): lax.ppermute(both[j], 'depth', [(i, (i + 2 * j) % 8) for i in range(8)])  10.9 us
    ppermute x1, waiting for transfers between devices, shards(): grad_down = lax.ppermute(sum_call(parts, terms[0]), ('depth', 'row'), perm)  10.8 us
    all_to_all x1, starting transfers between devices, shards(): wa = lax.all_to_all(columns_call(pos, down_weight), 'row', 0, 0)  10.4 us
    ppermute x3, starting transfers between devices, shards(): got = lax.ppermute(terms[j], 'row', [(i, (i + j) % 4) for i in range(4)])  9.82 us
    ppermute x1, starting transfers between devices, shards(): grad_down = lax.ppermute(sum_call(parts, terms[0]), ('depth', 'row'), perm)  6.97 us
  transfers between devices with their start and end apart: 14, of which 3 were waited for; matrix products, arithmetic and copies ran while one was open for 1% of the time, Pallas kernels for 9%

profile of v3, /device:TPU:4, one launch (start us, length us, event | category | flops | bytes accessed | tf_op | source)
XLA Modules:
  0.0 129.3 jit_solution(12744353180548481852)
XLA Ops:
  0.7 0.1 stack.23.pos
  0.7 2.0 %copy-done = bf16[224,8192]{1,0:T(8,128)(2,1)S(1)} copy-done((bf16[224,8192]{1,0:T(8,128)(2,1)S(1)}, bf16[224,8192]{1,0:T(8,128)(2,1)}, u32[]{:S(2)}) %copy-start) | copy-done | bytes 3670040
  2.8 2.0 %shard_map.67 = bf16[4,224,1024]{2,1,0:T(8,128)(2,1)} custom-call(s32[5]{0:T(128)S(1)} %stack.23.pos, bf16[224,8192]{1,0:T(8,128)(2,1)S(1)} %copy-done), custom_call_target="tpu_custom_call" | custom-call | bytes 3670016 | tf_op jit(solution)/shard_map/pallas_call | solution.py:32
  4.8 0.0 copy-start.3
  4.8 0.0 copy-start.1
  4.8 0.0 copy-start.2
  4.8 10.4 %all-to-all-start = ((bf16[4,224,1024]{2,1,0:T(8,128)(2,1)}), bf16[4,224,1024]{2,1,0:T(8,128)(2,1)}, u32[]{:S(2)}, u32[]{:S(2)}) async-start(bf16[4,224,1024]{2,1,0:T(8,128)(2,1)} %shard_map.67), calls=%async_computation | async-start | bytes 3670016 | tf_op jit(solution)/shard_map/all_to_all | solution.py:182
  15.2 29.1 %all-gather = bf16[2048,128]{1,0:T(8,128)(2,1)S(1)} all-gather(bf16[512,128]{1,0:T(8,128)(2,1)S(1)} %copy-done.3), channel_id=2, replica_groups={{0,4,8,12},{1,5,9,13},{2,6,10,14},{3,7,11,15},{16,20,24,28},{17,21,25,2..., dimensions={0}, use_global_device_ids=true | all-gather | bytes 655360 | tf_op jit(solution)/shard_map/all_gather | solution.py:185
  44.3 2.6 %collective-permute-start.1 = (bf16[4,512,128]{2,1,0:T(8,128)(2,1)S(1)}, bf16[4,512,128]{2,1,0:T(8,128)(2,1)S(1)}, u32[]{:S(2)}, u32[]{:S(2)}) collective-permute-start(bf16[4,512,128]{2,1,0:T(8,128)(2,1)S(1)} %bitcast.24), channel_id=1, source_target_pairs={{1,0},{2,1},{3,2},{4,3},{5,4},{6,5},{7,6},{8,7},{9,8},{10,9},{11,1... | collective-permute-start | bytes 1572872 | tf_op jit(solution)/shard_map/ppermute | solution.py:11
  46.9 3.2 %collective-permute-start.4 = (bf16[4,512,128]{2,1,0:T(8,128)(2,1)S(1)}, bf16[4,512,128]{2,1,0:T(8,128)(2,1)S(1)}, u32[]{:S(2)}, u32[]{:S(2)}) collective-permute-start(bf16[4,512,128]{2,1,0:T(8,128)(2,1)S(1)} %bitcast.25), channel_id=1, source_target_pairs={{15,0},{0,1},{1,2},{2,3},{3,4},{4,5},{5,6},{6,7},{7,8},{8,9},{9,10... | collective-permute-start | bytes 1572872 | tf_op jit(solution)/shard_map/ppermute | solution.py:11
  50.2 3.5 %collective-permute-start.2 = (bf16[2,512,128]{2,1,0:T(8,128)(2,1)S(1)}, bf16[2,512,128]{2,1,0:T(8,128)(2,1)S(1)}, u32[]{:S(2)}, u32[]{:S(2)}) collective-permute-start(bf16[2,512,128]{2,1,0:T(8,128)(2,1)S(1)} %get-tuple-element.22), channel_id=1, source_target_pairs={{2,0},{3,1},{4,2},{5,3},{6,4},{7,5},{8,6},{9,7},{10,8},{11,9},{12,... | collective-permute-start | bytes 786440 | tf_op jit(solution)/shard_map/ppermute | solution.py:11
  53.7 3.2 %collective-permute-start.3 = (bf16[2,512,128]{2,1,0:T(8,128)(2,1)S(1)}, bf16[2,512,128]{2,1,0:T(8,128)(2,1)S(1)}, u32[]{:S(2)}, u32[]{:S(2)}) collective-permute-start(bf16[2,512,128]{2,1,0:T(8,128)(2,1)S(1)} %get-tuple-element.21), channel_id=1, source_target_pairs={{14,0},{15,1},{0,2},{1,3},{2,4},{3,5},{4,6},{5,7},{6,8},{7,9},{8,1... | collective-permute-start | bytes 786440 | tf_op jit(solution)/shard_map/ppermute | solution.py:11
  57.0 0.1 shard_map.69
  57.1 13.2 %all-gather.1 = bf16[896,512]{1,0:T(8,128)(2,1)S(1)} all-gather(bf16[224,512]{1,0:T(8,128)(2,1)S(1)} %shard_map.69), channel_id=3, replica_groups=mesh['depth'=8,'row'=4,'col'=16] {'row'}, dimensions={0}, use_global_device_ids=true | all-gather | bytes 1146880 | tf_op jit(solution)/shard_map/all_gather | solution.py:191
  70.3 3.1 %shard_map.70 = bf16[4,224,1024]{2,1,0:T(8,128)(2,1)} custom-call(s32[5]{0:T(128)S(1)} %stack.23.pos, bf16[4,224,512]{2,1,0:T(8,128)(2,1)S(1)} %bitcast.16, bf16[4,224,512]{2,1,0:T(8,128)(2,1)S(1)} %bitcast.17, bf16[4,224,512]{2,1,0:T(8,128)(2,1)S(1)} %bitcast.18, bf16[4,224,512]{2,1,0:T(8,128)(2,1)S(1)} %bitcast.19, bf16[4,512,128]{2,1,0:T(8,128)(2,1)S(1)} %bitcast.28, ...), custom_call_target="tpu_custom_call" | custom-call | flops 939524096 | bytes 5242880 | tf_op jit(solution)/shard_map/pallas_call | solution.py:113
  73.4 1.9 %collective-permute-start.8 = (bf16[4,224,1024]{2,1,0:T(8,128)(2,1)}, bf16[4,224,1024]{2,1,0:T(8,128)(2,1)}, u32[]{:S(2)}, u32[]{:S(2)}) collective-permute-start(bf16[4,224,1024]{2,1,0:T(8,128)(2,1)} %shard_map.70), channel_id=1, source_target_pairs={{0,64},{64,0},{128,192},{192,128},{256,320},{320,256},{384,448},{4... | collective-permute-start | bytes 5505032 | tf_op jit(solution)/shard_map/ppermute | solution.py:15
  75.3 2.4 %collective-permute-start = (bf16[4,224,1024]{2,1,0:T(8,128)(2,1)}, bf16[4,224,1024]{2,1,0:T(8,128)(2,1)S(1)}, u32[]{:S(2)}, u32[]{:S(2)}) collective-permute-start(bf16[4,224,1024]{2,1,0:T(8,128)(2,1)} %all-to-all-done.wa), channel_id=1, source_target_pairs={{0,64},{64,0},{128,192},{192,128},{256,320},{320,256},{384,448},{4... | collective-permute-start | bytes 5505032 | tf_op jit(solution)/shard_map/ppermute | solution.py:15
  77.7 1.7 %collective-permute-done.8.refs_12_ = bf16[4,224,1024]{2,1,0:T(8,128)(2,1)} collective-permute-done((bf16[4,224,1024]{2,1,0:T(8,128)(2,1)}, bf16[4,224,1024]{2,1,0:T(8,128)(2,1)}, u32[]{:S(2)}, u32[]{:S(2)}) %collective-permute-start.8) | collective-permute-done | bytes 1835040 | tf_op jit(solution)/shard_map/ppermute | solution.py:15
  79.4 3.3 %shard_map.71 = (bf16[224,1024]{1,0:T(8,128)(2,1)S(1)}, bf16[224,1024]{1,0:T(8,128)(2,1)S(1)}, bf16[224,1024]{1,0:T(8,128)(2,1)S(1)}, bf16[224,1024]{1,0:T(8,128)(2,1)S(1)}) custom-call(s32[5]{0:T(128)S(1)} %stack.23.pos, bf16[4,224,512]{2,1,0:T(8,128)(2,1)S(1)} %bitcast.20, bf16[4,224,512]{2,1,0:T(8,128)(2,1)S(1)} %bitcast.21, ...), custom_call_target="tpu_custom_call" | custom-call | flops 939524096 | bytes 5242880 | tf_op jit(solution)/shard_map/pallas_call | solution.py:113
  82.7 3.5 %collective-permute-start.9 = (bf16[224,1024]{1,0:T(8,128)(2,1)S(1)}, bf16[224,1024]{1,0:T(8,128)(2,1)S(1)}, u32[]{:S(2)}, u32[]{:S(2)}) collective-permute-start(bf16[224,1024]{1,0:T(8,128)(2,1)S(1)} %get-tuple-element.16), channel_id=1, source_target_pairs={{0,128},{64,192},{128,256},{192,320},{256,384},{320,448},{384,0},{... | collective-permute-start | bytes 1376264 | tf_op jit(solution)/shard_map/ppermute | solution.py:198
  86.2 3.6 %collective-permute-start.10 = (bf16[224,1024]{1,0:T(8,128)(2,1)S(1)}, bf16[224,1024]{1,0:T(8,128)(2,1)S(1)}, u32[]{:S(2)}, u32[]{:S(2)}) collective-permute-start(bf16[224,1024]{1,0:T(8,128)(2,1)S(1)} %get-tuple-element.17), channel_id=1, source_target_pairs={{0,384},{64,448},{128,0},{192,64},{256,128},{320,192},{384,256},{4... | collective-permute-start | bytes 1376264 | tf_op jit(solution)/shard_map/ppermute | solution.py:198
  89.8 3.9 %collective-permute-start.11 = (bf16[224,1024]{1,0:T(8,128)(2,1)S(1)}, bf16[224,1024]{1,0:T(8,128)(2,1)S(1)}, u32[]{:S(2)}, u32[]{:S(2)}) collective-permute-start(bf16[224,1024]{1,0:T(8,128)(2,1)S(1)} %get-tuple-element.18), channel_id=1, source_target_pairs={{0,256},{64,320},{128,384},{192,448},{256,0},{320,64},{384,128},{4... | collective-permute-start | bytes 1376264 | tf_op jit(solution)/shard_map/ppermute | solution.py:198
  93.7 4.4 %shard_map.68 = (bf16[224,512]{1,0:T(8,128)(2,1)S(1)}, bf16[224,512]{1,0:T(8,128)(2,1)S(1)}, bf16[224,512]{1,0:T(8,128)(2,1)S(1)}, bf16[224,512]{1,0:T(8,128)(2,1)S(1)}) custom-call(s32[5]{0:T(128)S(1)} %stack.23.pos, bf16[4,224,1024]{2,1,0:T(8,128)(2,1)} %all-to-all-done.wa, bf16[4,224,1024]{2,1,0:T(8,128)(2,1)S(1)} %collective-permute-done.wb, ...), custom_call_target="tpu_custom_call" | custom-call | flops 1879048192 | bytes 7340032 | tf_op jit(solution)/shard_map/pallas_call | solution.py:163
  98.0 4.0 %collective-permute-start.7 = (bf16[224,512]{1,0:T(8,128)(2,1)S(1)}, bf16[224,512]{1,0:T(8,128)(2,1)S(1)}, u32[]{:S(2)}, u32[]{:S(2)}) collective-permute-start(bf16[224,512]{1,0:T(8,128)(2,1)S(1)} %get-tuple-element.14), channel_id=1, source_target_pairs={{0,32},{16,48},{32,0},{48,16},{1,33},{17,49},{33,1},{49,17},{2,34}... | collective-permute-start | bytes 688136 | tf_op jit(solution)/shard_map/ppermute | solution.py:212
  102.0 3.7 %collective-permute-start.6 = (bf16[224,512]{1,0:T(8,128)(2,1)S(1)}, bf16[224,512]{1,0:T(8,128)(2,1)S(1)}, u32[]{:S(2)}, u32[]{:S(2)}) collective-permute-start(bf16[224,512]{1,0:T(8,128)(2,1)S(1)} %get-tuple-element.13), channel_id=1, source_target_pairs={{0,48},{16,0},{32,16},{48,32},{1,49},{17,1},{33,17},{49,33},{2,50}... | collective-permute-start | bytes 688136 | tf_op jit(solution)/shard_map/ppermute | solution.py:212
  105.7 2.2 %collective-permute-start.5 = (bf16[224,512]{1,0:T(8,128)(2,1)S(1)}, bf16[224,512]{1,0:T(8,128)(2,1)S(1)}, u32[]{:S(2)}, u32[]{:S(2)}) collective-permute-start(bf16[224,512]{1,0:T(8,128)(2,1)S(1)} %get-tuple-element.12), channel_id=1, source_target_pairs={{0,16},{16,32},{32,48},{48,0},{1,17},{17,33},{33,49},{49,1},{2,18}... | collective-permute-start | bytes 688136 | tf_op jit(solution)/shard_map/ppermute | solution.py:212
  107.9 1.5 %collective-permute-done.11.d = bf16[224,1024]{1,0:T(8,128)(2,1)S(1)} collective-permute-done((bf16[224,1024]{1,0:T(8,128)(2,1)S(1)}, bf16[224,1024]{1,0:T(8,128)(2,1)S(1)}, u32[]{:S(2)}, u32[]{:S(2)}) %collective-permute-start.11) | collective-permute-done | bytes 458784 | tf_op jit(solution)/shard_map/ppermute | solution.py:198
  109.4 0.2 shard_map.72
  109.7 7.0 %collective-permute-start.12 = (bf16[224,1024]{1,0:T(8,128)(2,1)S(1)}, bf16[224,1024]{1,0:T(8,128)(2,1)S(1)}, u32[]{:S(2)}, u32[]{:S(2)}) collective-permute-start(bf16[224,1024]{1,0:T(8,128)(2,1)S(1)} %shard_map.72), channel_id=1, source_target_pairs={{0,0},{16,176},{32,288},{48,400},{64,64},{80,240},{96,352},{112,46... | collective-permute-start | bytes 1376264 | tf_op jit(solution)/shard_map/ppermute | solution.py:204
  116.7 1.1 fusion.8
  117.8 10.8 %collective-permute-done.12 = bf16[224,1024]{1,0:T(8,128)(2,1)S(1)} collective-permute-done((bf16[224,1024]{1,0:T(8,128)(2,1)S(1)}, bf16[224,1024]{1,0:T(8,128)(2,1)S(1)}, u32[]{:S(2)}, u32[]{:S(2)}) %collective-permute-start.12) | collective-permute-done | bytes 458784 | tf_op jit(solution)/shard_map/ppermute | solution.py:204
  128.6 0.8 copy.8
  (16 shorter events, 0.1 us)
Async XLA Ops:
  0.7 2.0 %copy-start = (bf16[224,8192]{1,0:T(8,128)(2,1)S(1)}, bf16[224,8192]{1,0:T(8,128)(2,1)}, u32[]{:S(2)}) copy-start(bf16[224,8192]{1,0:T(8,128)(2,1)} %w.1) | copy-start | bytes 11010052
  4.8 10.4 %copy-start.3 = (bf16[512,128]{1,0:T(8,128)(2,1)S(1)}, bf16[512,128]{1,0:T(8,128)(2,1)}, u32[]{:S(2)}) copy-start(bf16[512,128]{1,0:T(8,128)(2,1)} %param.4) | copy-start | bytes 393220
  4.8 52.2 %copy-start.1 = (bf16[512,224]{0,1:T(8,128)(2,1)S(1)}, bf16[512,224]{0,1:T(8,128)(2,1)}, u32[]{:S(2)}) copy-start(bf16[512,224]{0,1:T(8,128)(2,1)} %param.5) | copy-start | bytes 688132
  4.8 52.2 %copy-start.2 = (bf16[512,224]{0,1:T(8,128)(2,1)S(1)}, bf16[512,224]{0,1:T(8,128)(2,1)}, u32[]{:S(2)}) copy-start(bf16[512,224]{0,1:T(8,128)(2,1)} %param.6) | copy-start | bytes 688132
  4.8 70.5 %all-to-all-start = ((bf16[4,224,1024]{2,1,0:T(8,128)(2,1)}), bf16[4,224,1024]{2,1,0:T(8,128)(2,1)}, u32[]{:S(2)}, u32[]{:S(2)}) async-start(bf16[4,224,1024]{2,1,0:T(8,128)(2,1)} %shard_map.67), calls=%async_computation | async-start | bytes 3670016 | tf_op jit(solution)/shard_map/all_to_all | solution.py:182
  44.3 26.0 %collective-permute-start.1 = (bf16[4,512,128]{2,1,0:T(8,128)(2,1)S(1)}, bf16[4,512,128]{2,1,0:T(8,128)(2,1)S(1)}, u32[]{:S(2)}, u32[]{:S(2)}) collective-permute-start(bf16[4,512,128]{2,1,0:T(8,128)(2,1)S(1)} %bitcast.24), channel_id=1, source_target_pairs={{1,0},{2,1},{3,2},{4,3},{5,4},{6,5},{7,6},{8,7},{9,8},{10,9},{11,1... | collective-permute-start | bytes 1572872 | tf_op jit(solution)/shard_map/ppermute | solution.py:11
  46.9 23.4 %collective-permute-start.4 = (bf16[4,512,128]{2,1,0:T(8,128)(2,1)S(1)}, bf16[4,512,128]{2,1,0:T(8,128)(2,1)S(1)}, u32[]{:S(2)}, u32[]{:S(2)}) collective-permute-start(bf16[4,512,128]{2,1,0:T(8,128)(2,1)S(1)} %bitcast.25), channel_id=1, source_target_pairs={{15,0},{0,1},{1,2},{2,3},{3,4},{4,5},{5,6},{6,7},{7,8},{8,9},{9,10... | collective-permute-start | bytes 1572872 | tf_op jit(solution)/shard_map/ppermute | solution.py:11
  50.2 20.1 %collective-permute-start.2 = (bf16[2,512,128]{2,1,0:T(8,128)(2,1)S(1)}, bf16[2,512,128]{2,1,0:T(8,128)(2,1)S(1)}, u32[]{:S(2)}, u32[]{:S(2)}) collective-permute-start(bf16[2,512,128]{2,1,0:T(8,128)(2,1)S(1)} %get-tuple-element.22), channel_id=1, source_target_pairs={{2,0},{3,1},{4,2},{5,3},{6,4},{7,5},{8,6},{9,7},{10,8},{11,9},{12,... | collective-permute-start | bytes 786440 | tf_op jit(solution)/shard_map/ppermute | solution.py:11
  53.7 16.6 %collective-permute-start.3 = (bf16[2,512,128]{2,1,0:T(8,128)(2,1)S(1)}, bf16[2,512,128]{2,1,0:T(8,128)(2,1)S(1)}, u32[]{:S(2)}, u32[]{:S(2)}) collective-permute-start(bf16[2,512,128]{2,1,0:T(8,128)(2,1)S(1)} %get-tuple-element.21), channel_id=1, source_target_pairs={{14,0},{15,1},{0,2},{1,3},{2,4},{3,5},{4,6},{5,7},{6,8},{7,9},{8,1... | collective-permute-start | bytes 786440 | tf_op jit(solution)/shard_map/ppermute | solution.py:11
  73.4 6.0 %collective-permute-start.8 = (bf16[4,224,1024]{2,1,0:T(8,128)(2,1)}, bf16[4,224,1024]{2,1,0:T(8,128)(2,1)}, u32[]{:S(2)}, u32[]{:S(2)}) collective-permute-start(bf16[4,224,1024]{2,1,0:T(8,128)(2,1)} %shard_map.70), channel_id=1, source_target_pairs={{0,64},{64,0},{128,192},{192,128},{256,320},{320,256},{384,448},{4... | collective-permute-start | bytes 5505032 | tf_op jit(solution)/shard_map/ppermute | solution.py:15
  75.3 18.4 %collective-permute-start = (bf16[4,224,1024]{2,1,0:T(8,128)(2,1)}, bf16[4,224,1024]{2,1,0:T(8,128)(2,1)S(1)}, u32[]{:S(2)}, u32[]{:S(2)}) collective-permute-start(bf16[4,224,1024]{2,1,0:T(8,128)(2,1)} %all-to-all-done.wa), channel_id=1, source_target_pairs={{0,64},{64,0},{128,192},{192,128},{256,320},{320,256},{384,448},{4... | collective-permute-start | bytes 5505032 | tf_op jit(solution)/shard_map/ppermute | solution.py:15
  82.7 23.0 %collective-permute-start.9 = (bf16[224,1024]{1,0:T(8,128)(2,1)S(1)}, bf16[224,1024]{1,0:T(8,128)(2,1)S(1)}, u32[]{:S(2)}, u32[]{:S(2)}) collective-permute-start(bf16[224,1024]{1,0:T(8,128)(2,1)S(1)} %get-tuple-element.16), channel_id=1, source_target_pairs={{0,128},{64,192},{128,256},{192,320},{256,384},{320,448},{384,0},{... | collective-permute-start | bytes 1376264 | tf_op jit(solution)/shard_map/ppermute | solution.py:198
  86.2 21.7 %collective-permute-start.10 = (bf16[224,1024]{1,0:T(8,128)(2,1)S(1)}, bf16[224,1024]{1,0:T(8,128)(2,1)S(1)}, u32[]{:S(2)}, u32[]{:S(2)}) collective-permute-start(bf16[224,1024]{1,0:T(8,128)(2,1)S(1)} %get-tuple-element.17), channel_id=1, source_target_pairs={{0,384},{64,448},{128,0},{192,64},{256,128},{320,192},{384,256},{4... | collective-permute-start | bytes 1376264 | tf_op jit(solution)/shard_map/ppermute | solution.py:198
  89.8 19.7 %collective-permute-start.11 = (bf16[224,1024]{1,0:T(8,128)(2,1)S(1)}, bf16[224,1024]{1,0:T(8,128)(2,1)S(1)}, u32[]{:S(2)}, u32[]{:S(2)}) collective-permute-start(bf16[224,1024]{1,0:T(8,128)(2,1)S(1)} %get-tuple-element.18), channel_id=1, source_target_pairs={{0,256},{64,320},{128,384},{192,448},{256,0},{320,64},{384,128},{4... | collective-permute-start | bytes 1376264 | tf_op jit(solution)/shard_map/ppermute | solution.py:198
  98.0 18.6 %collective-permute-start.7 = (bf16[224,512]{1,0:T(8,128)(2,1)S(1)}, bf16[224,512]{1,0:T(8,128)(2,1)S(1)}, u32[]{:S(2)}, u32[]{:S(2)}) collective-permute-start(bf16[224,512]{1,0:T(8,128)(2,1)S(1)} %get-tuple-element.14), channel_id=1, source_target_pairs={{0,32},{16,48},{32,0},{48,16},{1,33},{17,49},{33,1},{49,17},{2,34}... | collective-permute-start | bytes 688136 | tf_op jit(solution)/shard_map/ppermute | solution.py:212
  102.0 14.6 %collective-permute-start.6 = (bf16[224,512]{1,0:T(8,128)(2,1)S(1)}, bf16[224,512]{1,0:T(8,128)(2,1)S(1)}, u32[]{:S(2)}, u32[]{:S(2)}) collective-permute-start(bf16[224,512]{1,0:T(8,128)(2,1)S(1)} %get-tuple-element.13), channel_id=1, source_target_pairs={{0,48},{16,0},{32,16},{48,32},{1,49},{17,1},{33,17},{49,33},{2,50}... | collective-permute-start | bytes 688136 | tf_op jit(solution)/shard_map/ppermute | solution.py:212
  105.7 10.9 %collective-permute-start.5 = (bf16[224,512]{1,0:T(8,128)(2,1)S(1)}, bf16[224,512]{1,0:T(8,128)(2,1)S(1)}, u32[]{:S(2)}, u32[]{:S(2)}) collective-permute-start(bf16[224,512]{1,0:T(8,128)(2,1)S(1)} %get-tuple-element.12), channel_id=1, source_target_pairs={{0,16},{16,32},{32,48},{48,0},{1,17},{17,33},{33,49},{49,1},{2,18}... | collective-permute-start | bytes 688136 | tf_op jit(solution)/shard_map/ppermute | solution.py:212
  109.7 18.9 %collective-permute-start.12 = (bf16[224,1024]{1,0:T(8,128)(2,1)S(1)}, bf16[224,1024]{1,0:T(8,128)(2,1)S(1)}, u32[]{:S(2)}, u32[]{:S(2)}) collective-permute-start(bf16[224,1024]{1,0:T(8,128)(2,1)S(1)} %shard_map.72), channel_id=1, source_target_pairs={{0,0},{16,176},{32,288},{48,400},{64,64},{80,240},{96,352},{112,46... | collective-permute-start | bytes 1376264 | tf_op jit(solution)/shard_map/ppermute | solution.py:204

commit v4 on v3

v4 whole, which is shorter than its diff:
```python
import jax
import jax.numpy as jnp
from jax import lax
from jax.experimental import pallas as pl
from jax.experimental.pallas import tpu as pltpu
from jax.sharding import PartitionSpec as P

ZG = [[g + 4 * j for j in range(4)] for g in range(4)]

def from_col(a, k):
    return lax.ppermute(a, "col", [((i + k) % 16, i) for i in range(16)])


def other_core(a):
    return lax.ppermute(a, "depth", [(i, i ^ 1) for i in range(8)])


def columns_kernel(pos, w, out, sems):
    d = out.shape[2]
    copies = [
        pltpu.make_async_copy(w.at[:, pl.ds(pl.multiple_of((2 * i + pos[0]) * d, d), d)], out.at[i], sems.at[i])
        for i in range(4)
    ]
    for c in copies:
        c.start()
    for c in copies:
        c.wait()


def columns_call(pos, w):
    f, d = w.shape
    return pl.pallas_call(
        columns_kernel,
        grid_spec=pltpu.PrefetchScalarGridSpec(
            num_scalar_prefetch=1,
            grid=(1,),
            in_specs=[pl.BlockSpec(memory_space=pltpu.HBM)],
            out_specs=pl.BlockSpec((4, f, d // 8), lambda g, p: (0, 0, 0)),
            scratch_shapes=[pltpu.SemaphoreType.DMA((4,))],
        ),
        out_shape=jax.ShapeDtypeStruct((4, f, d // 8), jnp.bfloat16),
        compiler_params=pltpu.CompilerParams(vmem_limit_bytes=12 * 1024 * 1024),
        cost_estimate=pl.CostEstimate(flops=0, bytes_accessed=2 * f * d, transcendentals=0),
    )(pos, w)


def hidden_kernel(gate, up, *refs):
    out = refs[-1]
    g = gate[...].astype(jnp.float32)
    out[...] = (g * jax.nn.sigmoid(g) * up[...].astype(jnp.float32)).astype(out.dtype)


def hidden_call(gate, up, *after):
    spec = pl.BlockSpec(gate.shape, lambda i: (0, 0))
    return pl.pallas_call(
        hidden_kernel,
        grid=(1,),
        in_specs=[spec, spec] + [pl.BlockSpec(memory_space=pl.ANY)] * len(after),
        out_specs=spec,
        out_shape=jax.ShapeDtypeStruct(gate.shape, jnp.bfloat16),
        compiler_params=pltpu.CompilerParams(vmem_limit_bytes=8 * 1024 * 1024),
        cost_estimate=pl.CostEstimate(flops=0, bytes_accessed=6 * gate.size, transcendentals=gate.size),
    )(gate, up, *after)


def gather_features(pos, sets, halves, cat):
    s0, s1, s2e, s2o, s3 = sets
    for k, h in enumerate(halves):
        for q in range(2):
            zg = 2 * h + q
            for r, block in enumerate((s0[zg], s1[zg], (s2e, s2o)[q][h], s3[zg])):
                at = pl.multiple_of(q * 512 + lax.rem(pos[2] + r, 4) * 128, 128)
                cat[k, :, pl.ds(at, 128)] = block


def rows_of(pos, hid, j):
    return hid[lax.rem(pos[4] + 4 + j - pos[3], 4)]


def away_kernel(pos, hid, s0, s1, s2e, s2o, s3, out, cat):
    gather_features(pos, (s0, s1, s2e, s2o, s3), (pos[1],), cat)
    for j in range(4):
        p = jnp.dot(rows_of(pos, hid, j), cat[0], preferred_element_type=jnp.float32)
        out[j] = (p * (1.0 / 64.0)).astype(out.dtype)


def both_kernel(pos, hid, s0, s1, s2e, s2o, s3, got, o0, o1, o2, o3, cat):
    gather_features(pos, (s0, s1, s2e, s2o, s3), (pos[0],), cat)
    for j, out in enumerate((o0, o1, o2, o3)):
        p = jnp.dot(rows_of(pos, hid, j), cat[0], preferred_element_type=jnp.float32)
        out[...] = (p * (1.0 / 64.0) + got[j].astype(jnp.float32)).astype(out.dtype)


def on_core(kernel, pos, args, out_shape, scratch, flops):
    vmem = pl.BlockSpec(memory_space=pltpu.VMEM)
    return pl.pallas_call(
        kernel,
        in_specs=[pl.BlockSpec(memory_space=pltpu.SMEM)] + [vmem] * len(args),
        out_specs=jax.tree.map(lambda _: vmem, out_shape, is_leaf=lambda o: not isinstance(o, list)),
        out_shape=out_shape,
        scratch_shapes=[scratch],
        compiler_params=pltpu.CompilerParams(vmem_limit_bytes=24 * 1024 * 1024),
        cost_estimate=pl.CostEstimate(flops=flops, bytes_accessed=5 * 1024 * 1024, transcendentals=0),
    )(pos, *args)


def partial_call(pos, hid, sets, got=None):
    n, f, t = hid.shape
    cat = pltpu.VMEM((1, t, 1024), jnp.bfloat16)
    flops = 2 * n * f * t * 1024
    if got is None:
        return on_core(away_kernel, pos, (hid, *sets), pltpu.VMEM((n, f, 1024), jnp.bfloat16), cat, flops)
    outs = [pltpu.VMEM((f, 1024), jnp.bfloat16)] * n
    return on_core(both_kernel, pos, (hid, *sets, got), outs, cat, flops)


def tie_kernel(a, after, out):
    pass


def tie(a, after):
    any_space = pl.BlockSpec(memory_space=pl.ANY)
    return pl.pallas_call(
        tie_kernel,
        in_specs=[any_space, any_space],
        out_specs=any_space,
        out_shape=jax.ShapeDtypeStruct(a.shape, a.dtype),
        input_output_aliases={0: 0},
        compiler_params=pltpu.CompilerParams(vmem_limit_bytes=1024 * 1024),
    )(a, after)


def sum_kernel(a, b, c, d, after, out):
    total = a[...].astype(jnp.float32) + b[...].astype(jnp.float32)
    out[...] = (total + c[...].astype(jnp.float32) + d[...].astype(jnp.float32)).astype(out.dtype)


def sum_call(parts, after):
    f, d = parts[0].shape
    return pl.pallas_call(
        sum_kernel,
        in_specs=[pl.BlockSpec(memory_space=pltpu.VMEM)] * 4 + [pl.BlockSpec(memory_space=pl.ANY)],
        out_specs=pl.BlockSpec(memory_space=pltpu.VMEM),
        out_shape=pltpu.VMEM((f, d), jnp.bfloat16),
        compiler_params=pltpu.CompilerParams(vmem_limit_bytes=8 * 1024 * 1024),
        cost_estimate=pl.CostEstimate(flops=3 * f * d, bytes_accessed=10 * f * d, transcendentals=0),
    )(*parts, after)


def hidden_grad_kernel(pos, wa, wb, s0, s1, s2e, s2o, s3, o0, o1, o2, o3, cat):
    gather_features(pos, (s0, s1, s2e, s2o, s3), (pos[0], pos[1]), cat)
    f = wa.shape[1]
    total = None
    for k, w in enumerate((wa, wb)):
        rows = jnp.concatenate([w[lax.rem(pos[3] + j, 4)] for j in range(4)], axis=0)
        part = lax.dot_general(rows, cat[k], (((1,), (1,)), ((), ())), preferred_element_type=jnp.float32)
        total = part if total is None else total + part
    for j, out in enumerate((o0, o1, o2, o3)):
        out[...] = total[j * f : j * f + f].astype(out.dtype)


def hidden_grad_call(pos, wa, wb, sets):
    n, f, d = wa.shape
    t = sets[0].shape[1]
    outs = [pltpu.VMEM((f, t), jnp.bfloat16)] * n
    cat = pltpu.VMEM((2, t, d), jnp.bfloat16)
    return on_core(hidden_grad_kernel, pos, (wa, wb, *sets), outs, cat, 4 * n * f * t * d)


def shards(grad_out, gate_pre, up_pre, down_weight):
    depth, row, col = lax.axis_index("depth"), lax.axis_index("row"), lax.axis_index("col")
    pos = jnp.stack([depth % 2, 1 - depth % 2, col % 4, row, depth // 2]).astype(jnp.int32)

    wa = lax.all_to_all(columns_call(pos, down_weight), "row", 0, 0)
    set0 = tie(lax.all_gather(grad_out, "col", axis=0, axis_index_groups=ZG), wa)
    set2 = (from_col(set0[0::2], 2), from_col(set0[1::2], -2))
    set1 = from_col(set0, 1)
    set3 = from_col(set0, -1)
    sets = (set0, set1, *set2, set3)

    hid = lax.all_gather(hidden_call(gate_pre.T, up_pre.T, set0), "row", axis=0)

    away = partial_call(pos, hid, sets)
    both = partial_call(pos, hid, sets, other_core(away))
    terms = hidden_grad_call(pos, wa, other_core(wa), sets)
    parts = [both[0]]
    for j in (1, 3, 2):
        parts.append(lax.ppermute(both[j], "depth", [(i, (i + 2 * j) % 8) for i in range(8)]))
    perm = []
    for y in range(4):
        for c in range(2):
            for x in range(4):
                perm.append(((2 * y + c) * 4 + x, (2 * x + c) * 4 + (y - x) % 4))
    grad_down = lax.ppermute(sum_call(parts, terms[0]), ("depth", "row"), perm)

    gate = gate_pre.T.astype(jnp.float32)
    upval = up_pre.T.astype(jnp.float32)
    sigma = jax.nn.sigmoid(gate)
    active = gate * sigma
    grad_hidden = terms[0].astype(jnp.float32)
    for j in (1, 3, 2):
        got = lax.ppermute(terms[j], "row", [(i, (i + j) % 4) for i in range(4)])
        grad_hidden = grad_hidden + got.astype(jnp.float32)
    grad_up = (grad_hidden * active).astype(jnp.bfloat16)
    grad_gate = (grad_hidden * upval * sigma * (1.0 + gate * (1.0 - sigma))).astype(jnp.bfloat16)
    return (grad_gate.T, grad_up.T, grad_down)


def solution(mesh):
    in_specs = (
        P("depth", ("row", "col")),
        P("depth", ("row", "col")),
        P("depth", ("row", "col")),
        P(("row", "col"), None),
    )
    out_specs = (P("depth", ("row", "col")), P("depth", ("row", "col")), P(("row", "col"), "depth"))
    return jax.shard_map(shards, mesh=mesh, in_specs=in_specs, out_specs=out_specs, check_vma=False)
```

time: 130 us -> 127 us (0.977)
  the two profiles are of different devices: /device:TPU:4 before, /device:TPU:36 now
where the time goes in v4:
time: 127 us
  starting transfers between devices  47.8 us (38%)
  blocking collectives  45.2 us (36%)
  waiting for transfers between devices  19.5 us (15%)
  Pallas kernels  7.77 us (6%)
  local copies, waits for them, and re-layouts  4.2 us (3%)
    all_gather x1, blocking collectives, shards(): lax.all_gather(grad_out, 'col', axis=0, axis_index_groups=ZG)  32 us
    ppermute x4, starting transfers between devices, from_col(): return lax.ppermute(a, 'col', [((i + k) % 16, i) for i in range(16)])  13.5 us
    all_gather x1, blocking collectives, shards(): hid = lax.all_gather(hidden_call(gate_pre.T, up_pre.T, set0), 'row', axis=0)  13.3 us
    ppermute x3, starting transfers between devices, shards(): lax.ppermute(both[j], 'depth', [(i, (i + 2 * j) % 8) for i in range(8)])  10.9 us
    ppermute x1, waiting for transfers between devices, shards(): grad_down = lax.ppermute(sum_call(parts, terms[0]), ('depth', 'row'), perm)  10.8 us
    ppermute x3, starting transfers between devices, shards(): got = lax.ppermute(terms[j], 'row', [(i, (i + j) % 4) for i in range(4)])  8.37 us
    pallas_call x3, Pallas kernels, on_core(): pl.pallas_call(kernel, in_specs=[pl.BlockSpec(memory_space=pltpu.SMEM)] +...  6.66 us
    ppermute x1, starting transfers between devices, shards(): grad_down = lax.ppermute(sum_call(parts, terms[0]), ('depth', 'row'), perm)  5.74 us
  transfers between devices with their start and end apart: 14, of which 4 were waited for; matrix products, arithmetic and copies ran while one was open for 1% of the time, Pallas kernels for 4%

profile of v4, /device:TPU:36, one launch (start us, length us, event | category | flops | bytes accessed | tf_op | source)
XLA Modules:
  0.0 126.5 jit_solution(11784771065390259008)
XLA Ops:
  0.7 0.1 stack.23.pos
  0.7 2.0 %copy-done.1 = bf16[224,8192]{1,0:T(8,128)(2,1)S(1)} copy-done((bf16[224,8192]{1,0:T(8,128)(2,1)S(1)}, bf16[224,8192]{1,0:T(8,128)(2,1)}, u32[]{:S(2)}) %copy-start.1) | copy-done | bytes 3670040
  2.8 0.8 shard_map.67
  3.6 1.3 copy-done
  4.8 4.9 %all-to-all-start = ((bf16[4,224,1024]{2,1,0:T(8,128)(2,1)}), bf16[4,224,1024]{2,1,0:T(8,128)(2,1)S(1)}, u32[]{:S(2)}, u32[]{:S(2)}) async-start(bf16[4,224,1024]{2,1,0:T(8,128)(2,1)} %copy-done), calls=%async_computation | async-start | bytes 3670016 | tf_op jit(solution)/shard_map/all_to_all | solution.py:174
  9.8 32.0 %all-gather = bf16[2048,128]{1,0:T(8,128)(2,1)S(1)} all-gather(bf16[512,128]{1,0:T(8,128)(2,1)S(1)} %copy-done.4), channel_id=2, replica_groups={{0,4,8,12},{1,5,9,13},{2,6,10,14},{3,7,11,15},{16,20,24,28},{17,21,25,2..., dimensions={0}, use_global_device_ids=true | all-gather | bytes 655360 | tf_op jit(solution)/shard_map/all_gather | solution.py:175
  41.7 0.0 all-to-all-done.after.wa
  41.8 2.4 %collective-permute-start.1 = (bf16[4,512,128]{2,1,0:T(8,128)(2,1)S(1)}, bf16[4,512,128]{2,1,0:T(8,128)(2,1)S(1)}, u32[]{:S(2)}, u32[]{:S(2)}) collective-permute-start(bf16[4,512,128]{2,1,0:T(8,128)(2,1)S(1)} %shard_map.68.s0.refs_0_), channel_id=1, source_target_pairs={{1,0},{2,1},{3,2},{4,3},{5,4},{6,5},{7,6},{8,7},{9,8},{10,9},{11,1... | collective-permute-start | bytes 1572872 | tf_op jit(solution)/shard_map/ppermute | solution.py:11
  44.2 3.6 %collective-permute-start.4 = (bf16[4,512,128]{2,1,0:T(8,128)(2,1)S(1)}, bf16[4,512,128]{2,1,0:T(8,128)(2,1)S(1)}, u32[]{:S(2)}, u32[]{:S(2)}) collective-permute-start(bf16[4,512,128]{2,1,0:T(8,128)(2,1)S(1)} %shard_map.68.s0.refs_0_), channel_id=1, source_target_pairs={{15,0},{0,1},{1,2},{2,3},{3,4},{4,5},{5,6},{6,7},{7,8},{8,9},{9,10... | collective-permute-start | bytes 1572872 | tf_op jit(solution)/shard_map/ppermute | solution.py:11
  47.8 5.6 %collective-permute-start.2 = (bf16[2,512,128]{2,1,0:T(8,128)(2,1)S(1)}, bf16[2,512,128]{2,1,0:T(8,128)(2,1)S(1)}, u32[]{:S(2)}, u32[]{:S(2)}) collective-permute-start(bf16[2,512,128]{2,1,0:T(8,128)(2,1)S(1)} %get-tuple-element.22), channel_id=1, source_target_pairs={{2,0},{3,1},{4,2},{5,3},{6,4},{7,5},{8,6},{9,7},{10,8},{11,9},{12,... | collective-permute-start | bytes 786440 | tf_op jit(solution)/shard_map/ppermute | solution.py:11
  53.4 1.9 %collective-permute-start.3 = (bf16[2,512,128]{2,1,0:T(8,128)(2,1)S(1)}, bf16[2,512,128]{2,1,0:T(8,128)(2,1)S(1)}, u32[]{:S(2)}, u32[]{:S(2)}) collective-permute-start(bf16[2,512,128]{2,1,0:T(8,128)(2,1)S(1)} %get-tuple-element.21), channel_id=1, source_target_pairs={{14,0},{15,1},{0,2},{1,3},{2,4},{3,5},{4,6},{5,7},{6,8},{7,9},{8,1... | collective-permute-start | bytes 786440 | tf_op jit(solution)/shard_map/ppermute | solution.py:11
  55.3 0.1 shard_map.70
  55.4 13.3 %all-gather.1 = bf16[896,512]{1,0:T(8,128)(2,1)S(1)} all-gather(bf16[224,512]{1,0:T(8,128)(2,1)S(1)} %shard_map.70), channel_id=3, replica_groups=mesh['depth'=8,'row'=4,'col'=16] {'row'}, dimensions={0}, use_global_device_ids=true | all-gather | bytes 1146880 | tf_op jit(solution)/shard_map/all_gather | solution.py:181
  68.7 2.9 %collective-permute-done.3.s2o = bf16[2,512,128]{2,1,0:T(8,128)(2,1)S(1)} collective-permute-done((bf16[2,512,128]{2,1,0:T(8,128)(2,1)S(1)}, bf16[2,512,128]{2,1,0:T(8,128)(2,1)S(1)}, u32[]{:S(2)}, u32[]{:S(2)}) %collective-permute-start.3) | collective-permute-done | bytes 262176 | tf_op jit(solution)/shard_map/ppermute | solution.py:11
  71.6 1.9 %shard_map.71 = bf16[4,224,1024]{2,1,0:T(8,128)(2,1)S(1)} custom-call(s32[5]{0:T(128)S(1)} %stack.23.pos, bf16[4,224,512]{2,1,0:T(8,128)(2,1)S(1)} %bitcast.17, bf16[4,512,128]{2,1,0:T(8,128)(2,1)S(1)} %shard_map.68.s0.refs_0_, bf16[4,512,128]{2,1,0:T(8,128)(2,1)S(1)} %collective-permute-done.1.s1, bf16[2,512,128]{2,1,0:T(8,128)(2,1)S(1)} %collective-permute-done.2.s2e, ...), custom_call_target="tpu_custom_call" | custom-call | flops 939524096 | bytes 5242880 | tf_op jit(solution)/shard_map/pallas_call | solution.py:96
  73.5 1.9 %collective-permute-start.8 = (bf16[4,224,1024]{2,1,0:T(8,128)(2,1)S(1)}, bf16[4,224,1024]{2,1,0:T(8,128)(2,1)S(1)}, u32[]{:S(2)}, u32[]{:S(2)}) collective-permute-start(bf16[4,224,1024]{2,1,0:T(8,128)(2,1)S(1)} %shard_map.71), channel_id=1, source_target_pairs={{0,64},{64,0},{128,192},{192,128},{256,320},{320,256},{384,448},{4... | collective-permute-start | bytes 5505032 | tf_op jit(solution)/shard_map/ppermute | solution.py:15
  75.4 2.4 %collective-permute-start = (bf16[4,224,1024]{2,1,0:T(8,128)(2,1)S(1)}, bf16[4,224,1024]{2,1,0:T(8,128)(2,1)S(1)}, u32[]{:S(2)}, u32[]{:S(2)}) collective-permute-start(bf16[4,224,1024]{2,1,0:T(8,128)(2,1)S(1)} %all-to-all-done.after.wa), channel_id=1, source_target_pairs={{0,64},{64,0},{128,192},{192,128},{256,320},{320,256},{384,448},{4... | collective-permute-start | bytes 5505032 | tf_op jit(solution)/shard_map/ppermute | solution.py:15
  77.8 1.3 %collective-permute-done.8.got = bf16[4,224,1024]{2,1,0:T(8,128)(2,1)S(1)} collective-permute-done((bf16[4,224,1024]{2,1,0:T(8,128)(2,1)S(1)}, bf16[4,224,1024]{2,1,0:T(8,128)(2,1)S(1)}, u32[]{:S(2)}, u32[]{:S(2)}) %collective-permute-start.8) | collective-permute-done | bytes 1835040 | tf_op jit(solution)/shard_map/ppermute | solution.py:15
  79.2 1.9 %shard_map.72 = (bf16[224,1024]{1,0:T(8,128)(2,1)S(1)}, bf16[224,1024]{1,0:T(8,128)(2,1)S(1)}, bf16[224,1024]{1,0:T(8,128)(2,1)S(1)}, bf16[224,1024]{1,0:T(8,128)(2,1)S(1)}) custom-call(s32[5]{0:T(128)S(1)} %stack.23.pos, bf16[4,224,512]{2,1,0:T(8,128)(2,1)S(1)} %bitcast.18, bf16[4,512,128]{2,1,0:T(8,128)(2,1)S(1)} %shard_map.68.s0.refs_0_, ...), custom_call_target="tpu_custom_call" | custom-call | flops 939524096 | bytes 5242880 | tf_op jit(solution)/shard_map/pallas_call | solution.py:96
  81.1 3.5 %collective-permute-start.9 = (bf16[224,1024]{1,0:T(8,128)(2,1)S(1)}, bf16[224,1024]{1,0:T(8,128)(2,1)S(1)}, u32[]{:S(2)}, u32[]{:S(2)}) collective-permute-start(bf16[224,1024]{1,0:T(8,128)(2,1)S(1)} %get-tuple-element.16), channel_id=1, source_target_pairs={{0,128},{64,192},{128,256},{192,320},{256,384},{320,448},{384,0},{... | collective-permute-start | bytes 1376264 | tf_op jit(solution)/shard_map/ppermute | solution.py:188
  84.6 3.6 %collective-permute-start.10 = (bf16[224,1024]{1,0:T(8,128)(2,1)S(1)}, bf16[224,1024]{1,0:T(8,128)(2,1)S(1)}, u32[]{:S(2)}, u32[]{:S(2)}) collective-permute-start(bf16[224,1024]{1,0:T(8,128)(2,1)S(1)} %get-tuple-element.17), channel_id=1, source_target_pairs={{0,384},{64,448},{128,0},{192,64},{256,128},{320,192},{384,256},{4... | collective-permute-start | bytes 1376264 | tf_op jit(solution)/shard_map/ppermute | solution.py:188
  88.2 3.9 %collective-permute-start.11 = (bf16[224,1024]{1,0:T(8,128)(2,1)S(1)}, bf16[224,1024]{1,0:T(8,128)(2,1)S(1)}, u32[]{:S(2)}, u32[]{:S(2)}) collective-permute-start(bf16[224,1024]{1,0:T(8,128)(2,1)S(1)} %get-tuple-element.18), channel_id=1, source_target_pairs={{0,256},{64,320},{128,384},{192,448},{256,0},{320,64},{384,128},{4... | collective-permute-start | bytes 1376264 | tf_op jit(solution)/shard_map/ppermute | solution.py:188
  92.1 2.9 %shard_map.69 = (bf16[224,512]{1,0:T(8,128)(2,1)S(1)}, bf16[224,512]{1,0:T(8,128)(2,1)S(1)}, bf16[224,512]{1,0:T(8,128)(2,1)S(1)}, bf16[224,512]{1,0:T(8,128)(2,1)S(1)}) custom-call(s32[5]{0:T(128)S(1)} %stack.23.pos, bf16[4,224,1024]{2,1,0:T(8,128)(2,1)S(1)} %all-to-all-done.after.wa, bf16[4,224,1024]{2,1,0:T(8,128)(2,1)S(1)} %collective-permute-done.wb, ...), custom_call_target="tpu_custom_call" | custom-call | flops 1879048192 | bytes 5242880 | tf_op jit(solution)/shard_map/pallas_call | solution.py:96
  95.0 1.9 %collective-permute-start.7 = (bf16[224,512]{1,0:T(8,128)(2,1)S(1)}, bf16[224,512]{1,0:T(8,128)(2,1)S(1)}, u32[]{:S(2)}, u32[]{:S(2)}) collective-permute-start(bf16[224,512]{1,0:T(8,128)(2,1)S(1)} %get-tuple-element.14), channel_id=1, source_target_pairs={{0,32},{16,48},{32,0},{48,16},{1,33},{17,49},{33,1},{49,17},{2,34}... | collective-permute-start | bytes 688136 | tf_op jit(solution)/shard_map/ppermute | solution.py:202
  96.9 4.5 %collective-permute-start.6 = (bf16[224,512]{1,0:T(8,128)(2,1)S(1)}, bf16[224,512]{1,0:T(8,128)(2,1)S(1)}, u32[]{:S(2)}, u32[]{:S(2)}) collective-permute-start(bf16[224,512]{1,0:T(8,128)(2,1)S(1)} %get-tuple-element.13), channel_id=1, source_target_pairs={{0,48},{16,0},{32,16},{48,32},{1,49},{17,1},{33,17},{49,33},{2,50}... | collective-permute-start | bytes 688136 | tf_op jit(solution)/shard_map/ppermute | solution.py:202
  101.4 1.9 %collective-permute-start.5 = (bf16[224,512]{1,0:T(8,128)(2,1)S(1)}, bf16[224,512]{1,0:T(8,128)(2,1)S(1)}, u32[]{:S(2)}, u32[]{:S(2)}) collective-permute-start(bf16[224,512]{1,0:T(8,128)(2,1)S(1)} %get-tuple-element.12), channel_id=1, source_target_pairs={{0,16},{16,32},{32,48},{48,0},{1,17},{17,33},{33,49},{49,1},{2,18}... | collective-permute-start | bytes 688136 | tf_op jit(solution)/shard_map/ppermute | solution.py:202
  103.4 4.5 %collective-permute-done.11.d = bf16[224,1024]{1,0:T(8,128)(2,1)S(1)} collective-permute-done((bf16[224,1024]{1,0:T(8,128)(2,1)S(1)}, bf16[224,1024]{1,0:T(8,128)(2,1)S(1)}, u32[]{:S(2)}, u32[]{:S(2)}) %collective-permute-start.11) | collective-permute-done | bytes 458784 | tf_op jit(solution)/shard_map/ppermute | solution.py:188
  107.8 0.2 shard_map.73
  108.1 5.7 %collective-permute-start.12 = (bf16[224,1024]{1,0:T(8,128)(2,1)S(1)}, bf16[224,1024]{1,0:T(8,128)(2,1)S(1)}, u32[]{:S(2)}, u32[]{:S(2)}) collective-permute-start(bf16[224,1024]{1,0:T(8,128)(2,1)S(1)} %shard_map.73), channel_id=1, source_target_pairs={{0,0},{16,176},{32,288},{48,400},{64,64},{80,240},{96,352},{112,46... | collective-permute-start | bytes 1376264 | tf_op jit(solution)/shard_map/ppermute | solution.py:194
  113.9 1.1 fusion.8
  115.0 10.8 %collective-permute-done.12 = bf16[224,1024]{1,0:T(8,128)(2,1)S(1)} collective-permute-done((bf16[224,1024]{1,0:T(8,128)(2,1)S(1)}, bf16[224,1024]{1,0:T(8,128)(2,1)S(1)}, u32[]{:S(2)}, u32[]{:S(2)}) %collective-permute-start.12) | collective-permute-done | bytes 458784 | tf_op jit(solution)/shard_map/ppermute | solution.py:194
  125.8 0.8 copy.10
  (19 shorter events, 0.1 us)
Async XLA Ops:
  0.7 2.0 %copy-start.1 = (bf16[224,8192]{1,0:T(8,128)(2,1)S(1)}, bf16[224,8192]{1,0:T(8,128)(2,1)}, u32[]{:S(2)}) copy-start(bf16[224,8192]{1,0:T(8,128)(2,1)} %w.1) | copy-start | bytes 11010052
  3.6 1.3 %copy-start = (bf16[4,224,1024]{2,1,0:T(8,128)(2,1)}, bf16[4,224,1024]{2,1,0:T(8,128)(2,1)S(1)}, u32[]{:S(2)}) copy-start(bf16[4,224,1024]{2,1,0:T(8,128)(2,1)S(1)} %shard_map.67) | copy-start | bytes 5505028
  4.8 4.9 %copy-start.4 = (bf16[512,128]{1,0:T(8,128)(2,1)S(1)}, bf16[512,128]{1,0:T(8,128)(2,1)}, u32[]{:S(2)}) copy-start(bf16[512,128]{1,0:T(8,128)(2,1)} %param.4) | copy-start | bytes 393220
  4.8 36.9 %all-to-all-start = ((bf16[4,224,1024]{2,1,0:T(8,128)(2,1)}), bf16[4,224,1024]{2,1,0:T(8,128)(2,1)S(1)}, u32[]{:S(2)}, u32[]{:S(2)}) async-start(bf16[4,224,1024]{2,1,0:T(8,128)(2,1)} %copy-done), calls=%async_computation | async-start | bytes 3670016 | tf_op jit(solution)/shard_map/all_to_all | solution.py:174
  41.7 13.6 %copy-start.2 = (bf16[512,224]{0,1:T(8,128)(2,1)S(1)}, bf16[512,224]{0,1:T(8,128)(2,1)}, u32[]{:S(2)}) copy-start(bf16[512,224]{0,1:T(8,128)(2,1)} %param.5) | copy-start | bytes 688132
  41.7 13.6 %copy-start.3 = (bf16[512,224]{0,1:T(8,128)(2,1)S(1)}, bf16[512,224]{0,1:T(8,128)(2,1)}, u32[]{:S(2)}) copy-start(bf16[512,224]{0,1:T(8,128)(2,1)} %param.6) | copy-start | bytes 688132
  41.8 29.9 %collective-permute-start.1 = (bf16[4,512,128]{2,1,0:T(8,128)(2,1)S(1)}, bf16[4,512,128]{2,1,0:T(8,128)(2,1)S(1)}, u32[]{:S(2)}, u32[]{:S(2)}) collective-permute-start(bf16[4,512,128]{2,1,0:T(8,128)(2,1)S(1)} %shard_map.68.s0.refs_0_), channel_id=1, source_target_pairs={{1,0},{2,1},{3,2},{4,3},{5,4},{6,5},{7,6},{8,7},{9,8},{10,9},{11,1... | collective-permute-start | bytes 1572872 | tf_op jit(solution)/shard_map/ppermute | solution.py:11
  44.2 27.5 %collective-permute-start.4 = (bf16[4,512,128]{2,1,0:T(8,128)(2,1)S(1)}, bf16[4,512,128]{2,1,0:T(8,128)(2,1)S(1)}, u32[]{:S(2)}, u32[]{:S(2)}) collective-permute-start(bf16[4,512,128]{2,1,0:T(8,128)(2,1)S(1)} %shard_map.68.s0.refs_0_), channel_id=1, source_target_pairs={{15,0},{0,1},{1,2},{2,3},{3,4},{4,5},{5,6},{6,7},{7,8},{8,9},{9,10... | collective-permute-start | bytes 1572872 | tf_op jit(solution)/shard_map/ppermute | solution.py:11
  47.8 20.9 %collective-permute-start.2 = (bf16[2,512,128]{2,1,0:T(8,128)(2,1)S(1)}, bf16[2,512,128]{2,1,0:T(8,128)(2,1)S(1)}, u32[]{:S(2)}, u32[]{:S(2)}) collective-permute-start(bf16[2,512,128]{2,1,0:T(8,128)(2,1)S(1)} %get-tuple-element.22), channel_id=1, source_target_pairs={{2,0},{3,1},{4,2},{5,3},{6,4},{7,5},{8,6},{9,7},{10,8},{11,9},{12,... | collective-permute-start | bytes 786440 | tf_op jit(solution)/shard_map/ppermute | solution.py:11
  53.4 18.3 %collective-permute-start.3 = (bf16[2,512,128]{2,1,0:T(8,128)(2,1)S(1)}, bf16[2,512,128]{2,1,0:T(8,128)(2,1)S(1)}, u32[]{:S(2)}, u32[]{:S(2)}) collective-permute-start(bf16[2,512,128]{2,1,0:T(8,128)(2,1)S(1)} %get-tuple-element.21), channel_id=1, source_target_pairs={{14,0},{15,1},{0,2},{1,3},{2,4},{3,5},{4,6},{5,7},{6,8},{7,9},{8,1... | collective-permute-start | bytes 786440 | tf_op jit(solution)/shard_map/ppermute | solution.py:11
  73.5 5.7 %collective-permute-start.8 = (bf16[4,224,1024]{2,1,0:T(8,128)(2,1)S(1)}, bf16[4,224,1024]{2,1,0:T(8,128)(2,1)S(1)}, u32[]{:S(2)}, u32[]{:S(2)}) collective-permute-start(bf16[4,224,1024]{2,1,0:T(8,128)(2,1)S(1)} %shard_map.71), channel_id=1, source_target_pairs={{0,64},{64,0},{128,192},{192,128},{256,320},{320,256},{384,448},{4... | collective-permute-start | bytes 5505032 | tf_op jit(solution)/shard_map/ppermute | solution.py:15
  75.4 16.6 %collective-permute-start = (bf16[4,224,1024]{2,1,0:T(8,128)(2,1)S(1)}, bf16[4,224,1024]{2,1,0:T(8,128)(2,1)S(1)}, u32[]{:S(2)}, u32[]{:S(2)}) collective-permute-start(bf16[4,224,1024]{2,1,0:T(8,128)(2,1)S(1)} %all-to-all-done.after.wa), channel_id=1, source_target_pairs={{0,64},{64,0},{128,192},{192,128},{256,320},{320,256},{384,448},{4... | collective-permute-start | bytes 5505032 | tf_op jit(solution)/shard_map/ppermute | solution.py:15
  81.1 20.3 %collective-permute-start.9 = (bf16[224,1024]{1,0:T(8,128)(2,1)S(1)}, bf16[224,1024]{1,0:T(8,128)(2,1)S(1)}, u32[]{:S(2)}, u32[]{:S(2)}) collective-permute-start(bf16[224,1024]{1,0:T(8,128)(2,1)S(1)} %get-tuple-element.16), channel_id=1, source_target_pairs={{0,128},{64,192},{128,256},{192,320},{256,384},{320,448},{384,0},{... | collective-permute-start | bytes 1376264 | tf_op jit(solution)/shard_map/ppermute | solution.py:188
  84.6 18.8 %collective-permute-start.10 = (bf16[224,1024]{1,0:T(8,128)(2,1)S(1)}, bf16[224,1024]{1,0:T(8,128)(2,1)S(1)}, u32[]{:S(2)}, u32[]{:S(2)}) collective-permute-start(bf16[224,1024]{1,0:T(8,128)(2,1)S(1)} %get-tuple-element.17), channel_id=1, source_target_pairs={{0,384},{64,448},{128,0},{192,64},{256,128},{320,192},{384,256},{4... | collective-permute-start | bytes 1376264 | tf_op jit(solution)/shard_map/ppermute | solution.py:188
  88.2 19.7 %collective-permute-start.11 = (bf16[224,1024]{1,0:T(8,128)(2,1)S(1)}, bf16[224,1024]{1,0:T(8,128)(2,1)S(1)}, u32[]{:S(2)}, u32[]{:S(2)}) collective-permute-start(bf16[224,1024]{1,0:T(8,128)(2,1)S(1)} %get-tuple-element.18), channel_id=1, source_target_pairs={{0,256},{64,320},{128,384},{192,448},{256,0},{320,64},{384,128},{4... | collective-permute-start | bytes 1376264 | tf_op jit(solution)/shard_map/ppermute | solution.py:188
  95.0 18.9 %collective-permute-start.7 = (bf16[224,512]{1,0:T(8,128)(2,1)S(1)}, bf16[224,512]{1,0:T(8,128)(2,1)S(1)}, u32[]{:S(2)}, u32[]{:S(2)}) collective-permute-start(bf16[224,512]{1,0:T(8,128)(2,1)S(1)} %get-tuple-element.14), channel_id=1, source_target_pairs={{0,32},{16,48},{32,0},{48,16},{1,33},{17,49},{33,1},{49,17},{2,34}... | collective-permute-start | bytes 688136 | tf_op jit(solution)/shard_map/ppermute | solution.py:202
  96.9 16.9 %collective-permute-start.6 = (bf16[224,512]{1,0:T(8,128)(2,1)S(1)}, bf16[224,512]{1,0:T(8,128)(2,1)S(1)}, u32[]{:S(2)}, u32[]{:S(2)}) collective-permute-start(bf16[224,512]{1,0:T(8,128)(2,1)S(1)} %get-tuple-element.13), channel_id=1, source_target_pairs={{0,48},{16,0},{32,16},{48,32},{1,49},{17,1},{33,17},{49,33},{2,50}... | collective-permute-start | bytes 688136 | tf_op jit(solution)/shard_map/ppermute | solution.py:202
  101.4 12.4 %collective-permute-start.5 = (bf16[224,512]{1,0:T(8,128)(2,1)S(1)}, bf16[224,512]{1,0:T(8,128)(2,1)S(1)}, u32[]{:S(2)}, u32[]{:S(2)}) collective-permute-start(bf16[224,512]{1,0:T(8,128)(2,1)S(1)} %get-tuple-element.12), channel_id=1, source_target_pairs={{0,16},{16,32},{32,48},{48,0},{1,17},{17,33},{33,49},{49,1},{2,18}... | collective-permute-start | bytes 688136 | tf_op jit(solution)/shard_map/ppermute | solution.py:202
  108.1 17.7 %collective-permute-start.12 = (bf16[224,1024]{1,0:T(8,128)(2,1)S(1)}, bf16[224,1024]{1,0:T(8,128)(2,1)S(1)}, u32[]{:S(2)}, u32[]{:S(2)}) collective-permute-start(bf16[224,1024]{1,0:T(8,128)(2,1)S(1)} %shard_map.73), channel_id=1, source_target_pairs={{0,0},{16,176},{32,288},{48,400},{64,64},{80,240},{96,352},{112,46... | collective-permute-start | bytes 1376264 | tf_op jit(solution)/shard_map/ppermute | solution.py:194

commit v5 on v4

--- a/solution.py
+++ b/solution.py
@@ -15,33 +15,32 @@
     return lax.ppermute(a, "depth", [(i, i ^ 1) for i in range(8)])
 
 
-def columns_kernel(pos, w, out, sems):
-    d = out.shape[2]
-    copies = [
-        pltpu.make_async_copy(w.at[:, pl.ds(pl.multiple_of((2 * i + pos[0]) * d, d), d)], out.at[i], sems.at[i])
-        for i in range(4)
-    ]
-    for c in copies:
-        c.start()
-    for c in copies:
-        c.wait()
+def columns_kernel(pos, w, out, held, sems):
+    n, _, d = out.shape
+    ins, outs = [], []
+    for i in range(n):
+        at = pl.multiple_of((2 * i + pos[0]) * d, d)
+        ins.append(pltpu.make_async_copy(w.at[:, pl.ds(at, d)], held.at[i], sems.at[0, i]))
+        outs.append(pltpu.make_async_copy(held.at[i], out.at[i], sems.at[1, i]))
+        ins[i].start()
+    for i in range(n):
+        ins[i].wait()
+        outs[i].start()
+    for i in range(n):
+        outs[i].wait()
 
 
 def columns_call(pos, w):
     f, d = w.shape
     return pl.pallas_call(
         columns_kernel,
-        grid_spec=pltpu.PrefetchScalarGridSpec(
-            num_scalar_prefetch=1,
-            grid=(1,),
-            in_specs=[pl.BlockSpec(memory_space=pltpu.HBM)],
-            out_specs=pl.BlockSpec((4, f, d // 8), lambda g, p: (0, 0, 0)),
-            scratch_shapes=[pltpu.SemaphoreType.DMA((4,))],
-        ),
-        out_shape=jax.ShapeDtypeStruct((4, f, d // 8), jnp.bfloat16),
+        in_specs=[pl.BlockSpec(memory_space=pltpu.SMEM), pl.BlockSpec(memory_space=pltpu.HBM)],
+        out_specs=pl.BlockSpec(memory_space=pltpu.HBM),
+        out_shape=pltpu.HBM((4, f, d // 8), jnp.bfloat16),
+        scratch_shapes=[pltpu.VMEM((4, f, d // 8), jnp.bfloat16), pltpu.SemaphoreType.DMA((2, 4))],
         compiler_params=pltpu.CompilerParams(vmem_limit_bytes=12 * 1024 * 1024),
         cost_estimate=pl.CostEstimate(flops=0, bytes_accessed=2 * f * d, transcendentals=0),
-    )(pos, w)
+    )(pos, pltpu.with_memory_space_constraint(w, pltpu.HBM))
 
 
 def hidden_kernel(gate, up, *refs):

time: 127 us -> 126 us (level)
  local copies, waits for them, and re-layouts: 4.2 us -> 0.9 us
  Pallas kernels: 7.77 us -> 9.84 us
    unnamed x11 -> x7, local copies, waits for them, and re-layouts: 4.08 us -> 0.78 us
    pallas_call x1, Pallas kernels: 0.76 us -> 2.9 us  [columns_call(): pl.pallas_call(columns_kernel, in_specs=[pl.BlockSpec(memory_space=pltpu....]
where the time goes in v5:
time: 126 us; the launch traced here: 125 us
  starting transfers between devices  47.8 us (38%)
  blocking collectives  45.2 us (36%)
  waiting for transfers between devices  19.6 us (16%)
  Pallas kernels  9.84 us (8%)
    all_gather x1, blocking collectives, shards(): lax.all_gather(grad_out, 'col', axis=0, axis_index_groups=ZG)  32 us
    ppermute x4, starting transfers between devices, from_col(): return lax.ppermute(a, 'col', [((i + k) % 16, i) for i in range(16)])  13.5 us
    all_gather x1, blocking collectives, shards(): hid = lax.all_gather(hidden_call(gate_pre.T, up_pre.T, set0), 'row', axis=0)  13.3 us
    ppermute x3, starting transfers between devices, shards(): lax.ppermute(both[j], 'depth', [(i, (i + 2 * j) % 8) for i in range(8)])  10.9 us
    ppermute x1, waiting for transfers between devices, shards(): grad_down = lax.ppermute(sum_call(parts, terms[0]), ('depth', 'row'), perm)  10.8 us
    ppermute x3, starting transfers between devices, shards(): got = lax.ppermute(terms[j], 'row', [(i, (i + j) % 4) for i in range(4)])  8.37 us
    pallas_call x3, Pallas kernels, on_core(): pl.pallas_call(kernel, in_specs=[pl.BlockSpec(memory_space=pltpu.SMEM)] +...  6.61 us
    ppermute x1, starting transfers between devices, shards(): grad_down = lax.ppermute(sum_call(parts, terms[0]), ('depth', 'row'), perm)  5.75 us
  transfers between devices with their start and end apart: 14, of which 4 were waited for; matrix products, arithmetic and copies ran while one was open for 1% of the time, Pallas kernels for 4%

profile of v5, /device:TPU:36, one launch (start us, length us, event | category | flops | bytes accessed | tf_op | source)
XLA Modules:
  0.0 125.3 jit_solution(184158897109560824)
XLA Ops:
  0.7 0.1 stack.23.pos
  0.7 2.9 %shard_map.67 = bf16[4,224,1024]{2,1,0:T(8,128)(2,1)} custom-call(s32[5]{0:T(128)S(1)} %stack.23.pos, bf16[224,8192]{1,0:T(8,128)(2,1)} %w.1), custom_call_target="tpu_custom_call" | custom-call | bytes 3670016 | tf_op jit(solution)/shard_map/pallas_call | solution.py:35
  3.6 0.0 copy-start.2
  3.7 4.9 %all-to-all-start = ((bf16[4,224,1024]{2,1,0:T(8,128)(2,1)}), bf16[4,224,1024]{2,1,0:T(8,128)(2,1)S(1)}, u32[]{:S(2)}, u32[]{:S(2)}) async-start(bf16[4,224,1024]{2,1,0:T(8,128)(2,1)} %shard_map.67), calls=%async_computation | async-start | bytes 3670016 | tf_op jit(solution)/shard_map/all_to_all | solution.py:173
  8.6 32.0 %all-gather = bf16[2048,128]{1,0:T(8,128)(2,1)S(1)} all-gather(bf16[512,128]{1,0:T(8,128)(2,1)S(1)} %copy-done.2), channel_id=2, replica_groups={{0,4,8,12},{1,5,9,13},{2,6,10,14},{3,7,11,15},{16,20,24,28},{17,21,25,2..., dimensions={0}, use_global_device_ids=true | all-gather | bytes 655360 | tf_op jit(solution)/shard_map/all_gather | solution.py:174
  40.6 0.0 all-to-all-done.after.wa
  40.6 2.4 %collective-permute-start.1 = (bf16[4,512,128]{2,1,0:T(8,128)(2,1)S(1)}, bf16[4,512,128]{2,1,0:T(8,128)(2,1)S(1)}, u32[]{:S(2)}, u32[]{:S(2)}) collective-permute-start(bf16[4,512,128]{2,1,0:T(8,128)(2,1)S(1)} %shard_map.68.s0.refs_0_), channel_id=1, source_target_pairs={{1,0},{2,1},{3,2},{4,3},{5,4},{6,5},{7,6},{8,7},{9,8},{10,9},{11,1... | collective-permute-start | bytes 1572872 | tf_op jit(solution)/shard_map/ppermute | solution.py:11
  43.0 3.6 %collective-permute-start.4 = (bf16[4,512,128]{2,1,0:T(8,128)(2,1)S(1)}, bf16[4,512,128]{2,1,0:T(8,128)(2,1)S(1)}, u32[]{:S(2)}, u32[]{:S(2)}) collective-permute-start(bf16[4,512,128]{2,1,0:T(8,128)(2,1)S(1)} %shard_map.68.s0.refs_0_), channel_id=1, source_target_pairs={{15,0},{0,1},{1,2},{2,3},{3,4},{4,5},{5,6},{6,7},{7,8},{8,9},{9,10... | collective-permute-start | bytes 1572872 | tf_op jit(solution)/shard_map/ppermute | solution.py:11
  46.6 5.6 %collective-permute-start.2 = (bf16[2,512,128]{2,1,0:T(8,128)(2,1)S(1)}, bf16[2,512,128]{2,1,0:T(8,128)(2,1)S(1)}, u32[]{:S(2)}, u32[]{:S(2)}) collective-permute-start(bf16[2,512,128]{2,1,0:T(8,128)(2,1)S(1)} %get-tuple-element.22), channel_id=1, source_target_pairs={{2,0},{3,1},{4,2},{5,3},{6,4},{7,5},{8,6},{9,7},{10,8},{11,9},{12,... | collective-permute-start | bytes 786440 | tf_op jit(solution)/shard_map/ppermute | solution.py:11
  52.2 1.9 %collective-permute-start.3 = (bf16[2,512,128]{2,1,0:T(8,128)(2,1)S(1)}, bf16[2,512,128]{2,1,0:T(8,128)(2,1)S(1)}, u32[]{:S(2)}, u32[]{:S(2)}) collective-permute-start(bf16[2,512,128]{2,1,0:T(8,128)(2,1)S(1)} %get-tuple-element.21), channel_id=1, source_target_pairs={{14,0},{15,1},{0,2},{1,3},{2,4},{3,5},{4,6},{5,7},{6,8},{7,9},{8,1... | collective-permute-start | bytes 786440 | tf_op jit(solution)/shard_map/ppermute | solution.py:11
  54.2 0.1 shard_map.70
  54.3 13.3 %all-gather.1 = bf16[896,512]{1,0:T(8,128)(2,1)S(1)} all-gather(bf16[224,512]{1,0:T(8,128)(2,1)S(1)} %shard_map.70), channel_id=3, replica_groups=mesh['depth'=8,'row'=4,'col'=16] {'row'}, dimensions={0}, use_global_device_ids=true | all-gather | bytes 1146880 | tf_op jit(solution)/shard_map/all_gather | solution.py:180
  67.5 0.0 collective-permute-done.2.s2e
  67.5 2.9 %collective-permute-done.3.s2o = bf16[2,512,128]{2,1,0:T(8,128)(2,1)S(1)} collective-permute-done((bf16[2,512,128]{2,1,0:T(8,128)(2,1)S(1)}, bf16[2,512,128]{2,1,0:T(8,128)(2,1)S(1)}, u32[]{:S(2)}, u32[]{:S(2)}) %collective-permute-start.3) | collective-permute-done | bytes 262176 | tf_op jit(solution)/shard_map/ppermute | solution.py:11
  70.5 1.9 %shard_map.71 = bf16[4,224,1024]{2,1,0:T(8,128)(2,1)S(1)} custom-call(s32[5]{0:T(128)S(1)} %stack.23.pos, bf16[4,224,512]{2,1,0:T(8,128)(2,1)S(1)} %bitcast.17, bf16[4,512,128]{2,1,0:T(8,128)(2,1)S(1)} %shard_map.68.s0.refs_0_, bf16[4,512,128]{2,1,0:T(8,128)(2,1)S(1)} %collective-permute-done.1.s1, bf16[2,512,128]{2,1,0:T(8,128)(2,1)S(1)} %collective-permute-done.2.s2e, ...), custom_call_target="tpu_custom_call" | custom-call | flops 939524096 | bytes 5242880 | tf_op jit(solution)/shard_map/pallas_call | solution.py:95
  72.3 1.9 %collective-permute-start.8 = (bf16[4,224,1024]{2,1,0:T(8,128)(2,1)S(1)}, bf16[4,224,1024]{2,1,0:T(8,128)(2,1)S(1)}, u32[]{:S(2)}, u32[]{:S(2)}) collective-permute-start(bf16[4,224,1024]{2,1,0:T(8,128)(2,1)S(1)} %shard_map.71), channel_id=1, source_target_pairs={{0,64},{64,0},{128,192},{192,128},{256,320},{320,256},{384,448},{4... | collective-permute-start | bytes 5505032 | tf_op jit(solution)/shard_map/ppermute | solution.py:15
  74.3 2.4 %collective-permute-start = (bf16[4,224,1024]{2,1,0:T(8,128)(2,1)S(1)}, bf16[4,224,1024]{2,1,0:T(8,128)(2,1)S(1)}, u32[]{:S(2)}, u32[]{:S(2)}) collective-permute-start(bf16[4,224,1024]{2,1,0:T(8,128)(2,1)S(1)} %all-to-all-done.after.wa), channel_id=1, source_target_pairs={{0,64},{64,0},{128,192},{192,128},{256,320},{320,256},{384,448},{4... | collective-permute-start | bytes 5505032 | tf_op jit(solution)/shard_map/ppermute | solution.py:15
  76.7 1.3 %collective-permute-done.8.got = bf16[4,224,1024]{2,1,0:T(8,128)(2,1)S(1)} collective-permute-done((bf16[4,224,1024]{2,1,0:T(8,128)(2,1)S(1)}, bf16[4,224,1024]{2,1,0:T(8,128)(2,1)S(1)}, u32[]{:S(2)}, u32[]{:S(2)}) %collective-permute-start.8) | collective-permute-done | bytes 1835040 | tf_op jit(solution)/shard_map/ppermute | solution.py:15
  78.0 1.9 %shard_map.72 = (bf16[224,1024]{1,0:T(8,128)(2,1)S(1)}, bf16[224,1024]{1,0:T(8,128)(2,1)S(1)}, bf16[224,1024]{1,0:T(8,128)(2,1)S(1)}, bf16[224,1024]{1,0:T(8,128)(2,1)S(1)}) custom-call(s32[5]{0:T(128)S(1)} %stack.23.pos, bf16[4,224,512]{2,1,0:T(8,128)(2,1)S(1)} %bitcast.18, bf16[4,512,128]{2,1,0:T(8,128)(2,1)S(1)} %shard_map.68.s0.refs_0_, ...), custom_call_target="tpu_custom_call" | custom-call | flops 939524096 | bytes 5242880 | tf_op jit(solution)/shard_map/pallas_call | solution.py:95
  79.9 3.5 %collective-permute-start.9 = (bf16[224,1024]{1,0:T(8,128)(2,1)S(1)}, bf16[224,1024]{1,0:T(8,128)(2,1)S(1)}, u32[]{:S(2)}, u32[]{:S(2)}) collective-permute-start(bf16[224,1024]{1,0:T(8,128)(2,1)S(1)} %get-tuple-element.16), channel_id=1, source_target_pairs={{0,128},{64,192},{128,256},{192,320},{256,384},{320,448},{384,0},{... | collective-permute-start | bytes 1376264 | tf_op jit(solution)/shard_map/ppermute | solution.py:187
  83.4 3.6 %collective-permute-start.10 = (bf16[224,1024]{1,0:T(8,128)(2,1)S(1)}, bf16[224,1024]{1,0:T(8,128)(2,1)S(1)}, u32[]{:S(2)}, u32[]{:S(2)}) collective-permute-start(bf16[224,1024]{1,0:T(8,128)(2,1)S(1)} %get-tuple-element.17), channel_id=1, source_target_pairs={{0,384},{64,448},{128,0},{192,64},{256,128},{320,192},{384,256},{4... | collective-permute-start | bytes 1376264 | tf_op jit(solution)/shard_map/ppermute | solution.py:187
  87.0 3.9 %collective-permute-start.11 = (bf16[224,1024]{1,0:T(8,128)(2,1)S(1)}, bf16[224,1024]{1,0:T(8,128)(2,1)S(1)}, u32[]{:S(2)}, u32[]{:S(2)}) collective-permute-start(bf16[224,1024]{1,0:T(8,128)(2,1)S(1)} %get-tuple-element.18), channel_id=1, source_target_pairs={{0,256},{64,320},{128,384},{192,448},{256,0},{320,64},{384,128},{4... | collective-permute-start | bytes 1376264 | tf_op jit(solution)/shard_map/ppermute | solution.py:187
  90.9 2.9 %shard_map.69 = (bf16[224,512]{1,0:T(8,128)(2,1)S(1)}, bf16[224,512]{1,0:T(8,128)(2,1)S(1)}, bf16[224,512]{1,0:T(8,128)(2,1)S(1)}, bf16[224,512]{1,0:T(8,128)(2,1)S(1)}) custom-call(s32[5]{0:T(128)S(1)} %stack.23.pos, bf16[4,224,1024]{2,1,0:T(8,128)(2,1)S(1)} %all-to-all-done.after.wa, bf16[4,224,1024]{2,1,0:T(8,128)(2,1)S(1)} %collective-permute-done.wb, ...), custom_call_target="tpu_custom_call" | custom-call | flops 1879048192 | bytes 5242880 | tf_op jit(solution)/shard_map/pallas_call | solution.py:95
  93.8 1.9 %collective-permute-start.7 = (bf16[224,512]{1,0:T(8,128)(2,1)S(1)}, bf16[224,512]{1,0:T(8,128)(2,1)S(1)}, u32[]{:S(2)}, u32[]{:S(2)}) collective-permute-start(bf16[224,512]{1,0:T(8,128)(2,1)S(1)} %get-tuple-element.14), channel_id=1, source_target_pairs={{0,32},{16,48},{32,0},{48,16},{1,33},{17,49},{33,1},{49,17},{2,34}... | collective-permute-start | bytes 688136 | tf_op jit(solution)/shard_map/ppermute | solution.py:201
  95.7 4.5 %collective-permute-start.6 = (bf16[224,512]{1,0:T(8,128)(2,1)S(1)}, bf16[224,512]{1,0:T(8,128)(2,1)S(1)}, u32[]{:S(2)}, u32[]{:S(2)}) collective-permute-start(bf16[224,512]{1,0:T(8,128)(2,1)S(1)} %get-tuple-element.13), channel_id=1, source_target_pairs={{0,48},{16,0},{32,16},{48,32},{1,49},{17,1},{33,17},{49,33},{2,50}... | collective-permute-start | bytes 688136 | tf_op jit(solution)/shard_map/ppermute | solution.py:201
  100.2 1.9 %collective-permute-start.5 = (bf16[224,512]{1,0:T(8,128)(2,1)S(1)}, bf16[224,512]{1,0:T(8,128)(2,1)S(1)}, u32[]{:S(2)}, u32[]{:S(2)}) collective-permute-start(bf16[224,512]{1,0:T(8,128)(2,1)S(1)} %get-tuple-element.12), channel_id=1, source_target_pairs={{0,16},{16,32},{32,48},{48,0},{1,17},{17,33},{33,49},{49,1},{2,18}... | collective-permute-start | bytes 688136 | tf_op jit(solution)/shard_map/ppermute | solution.py:201
  102.2 4.5 %collective-permute-done.11.d = bf16[224,1024]{1,0:T(8,128)(2,1)S(1)} collective-permute-done((bf16[224,1024]{1,0:T(8,128)(2,1)S(1)}, bf16[224,1024]{1,0:T(8,128)(2,1)S(1)}, u32[]{:S(2)}, u32[]{:S(2)}) %collective-permute-start.11) | collective-permute-done | bytes 458784 | tf_op jit(solution)/shard_map/ppermute | solution.py:187
  106.7 0.2 shard_map.73
  106.9 5.8 %collective-permute-start.12 = (bf16[224,1024]{1,0:T(8,128)(2,1)S(1)}, bf16[224,1024]{1,0:T(8,128)(2,1)S(1)}, u32[]{:S(2)}, u32[]{:S(2)}) collective-permute-start(bf16[224,1024]{1,0:T(8,128)(2,1)S(1)} %shard_map.73), channel_id=1, source_target_pairs={{0,0},{16,176},{32,288},{48,400},{64,64},{80,240},{96,352},{112,46... | collective-permute-start | bytes 1376264 | tf_op jit(solution)/shard_map/ppermute | solution.py:193
  112.7 1.1 fusion.8
  113.8 10.8 %collective-permute-done.12 = bf16[224,1024]{1,0:T(8,128)(2,1)S(1)} collective-permute-done((bf16[224,1024]{1,0:T(8,128)(2,1)S(1)}, bf16[224,1024]{1,0:T(8,128)(2,1)S(1)}, u32[]{:S(2)}, u32[]{:S(2)}) %collective-permute-start.12) | collective-permute-done | bytes 458784 | tf_op jit(solution)/shard_map/ppermute | solution.py:193
  124.6 0.8 copy.10
  (15 shorter events, 0.1 us)
Async XLA Ops:
  3.6 5.0 %copy-start.2 = (bf16[512,128]{1,0:T(8,128)(2,1)S(1)}, bf16[512,128]{1,0:T(8,128)(2,1)}, u32[]{:S(2)}) copy-start(bf16[512,128]{1,0:T(8,128)(2,1)} %param.4) | copy-start | bytes 393220
  3.7 36.9 %all-to-all-start = ((bf16[4,224,1024]{2,1,0:T(8,128)(2,1)}), bf16[4,224,1024]{2,1,0:T(8,128)(2,1)S(1)}, u32[]{:S(2)}, u32[]{:S(2)}) async-start(bf16[4,224,1024]{2,1,0:T(8,128)(2,1)} %shard_map.67), calls=%async_computation | async-start | bytes 3670016 | tf_op jit(solution)/shard_map/all_to_all | solution.py:173
  40.6 13.5 %copy-start = (bf16[512,224]{0,1:T(8,128)(2,1)S(1)}, bf16[512,224]{0,1:T(8,128)(2,1)}, u32[]{:S(2)}) copy-start(bf16[512,224]{0,1:T(8,128)(2,1)} %param.5) | copy-start | bytes 688132
  40.6 13.6 %copy-start.1 = (bf16[512,224]{0,1:T(8,128)(2,1)S(1)}, bf16[512,224]{0,1:T(8,128)(2,1)}, u32[]{:S(2)}) copy-start(bf16[512,224]{0,1:T(8,128)(2,1)} %param.6) | copy-start | bytes 688132
  40.6 29.9 %collective-permute-start.1 = (bf16[4,512,128]{2,1,0:T(8,128)(2,1)S(1)}, bf16[4,512,128]{2,1,0:T(8,128)(2,1)S(1)}, u32[]{:S(2)}, u32[]{:S(2)}) collective-permute-start(bf16[4,512,128]{2,1,0:T(8,128)(2,1)S(1)} %shard_map.68.s0.refs_0_), channel_id=1, source_target_pairs={{1,0},{2,1},{3,2},{4,3},{5,4},{6,5},{7,6},{8,7},{9,8},{10,9},{11,1... | collective-permute-start | bytes 1572872 | tf_op jit(solution)/shard_map/ppermute | solution.py:11
  43.0 27.4 %collective-permute-start.4 = (bf16[4,512,128]{2,1,0:T(8,128)(2,1)S(1)}, bf16[4,512,128]{2,1,0:T(8,128)(2,1)S(1)}, u32[]{:S(2)}, u32[]{:S(2)}) collective-permute-start(bf16[4,512,128]{2,1,0:T(8,128)(2,1)S(1)} %shard_map.68.s0.refs_0_), channel_id=1, source_target_pairs={{15,0},{0,1},{1,2},{2,3},{3,4},{4,5},{5,6},{6,7},{7,8},{8,9},{9,10... | collective-permute-start | bytes 1572872 | tf_op jit(solution)/shard_map/ppermute | solution.py:11
  46.6 20.9 %collective-permute-start.2 = (bf16[2,512,128]{2,1,0:T(8,128)(2,1)S(1)}, bf16[2,512,128]{2,1,0:T(8,128)(2,1)S(1)}, u32[]{:S(2)}, u32[]{:S(2)}) collective-permute-start(bf16[2,512,128]{2,1,0:T(8,128)(2,1)S(1)} %get-tuple-element.22), channel_id=1, source_target_pairs={{2,0},{3,1},{4,2},{5,3},{6,4},{7,5},{8,6},{9,7},{10,8},{11,9},{12,... | collective-permute-start | bytes 786440 | tf_op jit(solution)/shard_map/ppermute | solution.py:11
  52.2 18.3 %collective-permute-start.3 = (bf16[2,512,128]{2,1,0:T(8,128)(2,1)S(1)}, bf16[2,512,128]{2,1,0:T(8,128)(2,1)S(1)}, u32[]{:S(2)}, u32[]{:S(2)}) collective-permute-start(bf16[2,512,128]{2,1,0:T(8,128)(2,1)S(1)} %get-tuple-element.21), channel_id=1, source_target_pairs={{14,0},{15,1},{0,2},{1,3},{2,4},{3,5},{4,6},{5,7},{6,8},{7,9},{8,1... | collective-permute-start | bytes 786440 | tf_op jit(solution)/shard_map/ppermute | solution.py:11
  72.3 5.7 %collective-permute-start.8 = (bf16[4,224,1024]{2,1,0:T(8,128)(2,1)S(1)}, bf16[4,224,1024]{2,1,0:T(8,128)(2,1)S(1)}, u32[]{:S(2)}, u32[]{:S(2)}) collective-permute-start(bf16[4,224,1024]{2,1,0:T(8,128)(2,1)S(1)} %shard_map.71), channel_id=1, source_target_pairs={{0,64},{64,0},{128,192},{192,128},{256,320},{320,256},{384,448},{4... | collective-permute-start | bytes 5505032 | tf_op jit(solution)/shard_map/ppermute | solution.py:15
  74.3 16.6 %collective-permute-start = (bf16[4,224,1024]{2,1,0:T(8,128)(2,1)S(1)}, bf16[4,224,1024]{2,1,0:T(8,128)(2,1)S(1)}, u32[]{:S(2)}, u32[]{:S(2)}) collective-permute-start(bf16[4,224,1024]{2,1,0:T(8,128)(2,1)S(1)} %all-to-all-done.after.wa), channel_id=1, source_target_pairs={{0,64},{64,0},{128,192},{192,128},{256,320},{320,256},{384,448},{4... | collective-permute-start | bytes 5505032 | tf_op jit(solution)/shard_map/ppermute | solution.py:15
  79.9 20.3 %collective-permute-start.9 = (bf16[224,1024]{1,0:T(8,128)(2,1)S(1)}, bf16[224,1024]{1,0:T(8,128)(2,1)S(1)}, u32[]{:S(2)}, u32[]{:S(2)}) collective-permute-start(bf16[224,1024]{1,0:T(8,128)(2,1)S(1)} %get-tuple-element.16), channel_id=1, source_target_pairs={{0,128},{64,192},{128,256},{192,320},{256,384},{320,448},{384,0},{... | collective-permute-start | bytes 1376264 | tf_op jit(solution)/shard_map/ppermute | solution.py:187
  83.4 18.8 %collective-permute-start.10 = (bf16[224,1024]{1,0:T(8,128)(2,1)S(1)}, bf16[224,1024]{1,0:T(8,128)(2,1)S(1)}, u32[]{:S(2)}, u32[]{:S(2)}) collective-permute-start(bf16[224,1024]{1,0:T(8,128)(2,1)S(1)} %get-tuple-element.17), channel_id=1, source_target_pairs={{0,384},{64,448},{128,0},{192,64},{256,128},{320,192},{384,256},{4... | collective-permute-start | bytes 1376264 | tf_op jit(solution)/shard_map/ppermute | solution.py:187
  87.0 19.7 %collective-permute-start.11 = (bf16[224,1024]{1,0:T(8,128)(2,1)S(1)}, bf16[224,1024]{1,0:T(8,128)(2,1)S(1)}, u32[]{:S(2)}, u32[]{:S(2)}) collective-permute-start(bf16[224,1024]{1,0:T(8,128)(2,1)S(1)} %get-tuple-element.18), channel_id=1, source_target_pairs={{0,256},{64,320},{128,384},{192,448},{256,0},{320,64},{384,128},{4... | collective-permute-start | bytes 1376264 | tf_op jit(solution)/shard_map/ppermute | solution.py:187
  93.8 18.9 %collective-permute-start.7 = (bf16[224,512]{1,0:T(8,128)(2,1)S(1)}, bf16[224,512]{1,0:T(8,128)(2,1)S(1)}, u32[]{:S(2)}, u32[]{:S(2)}) collective-permute-start(bf16[224,512]{1,0:T(8,128)(2,1)S(1)} %get-tuple-element.14), channel_id=1, source_target_pairs={{0,32},{16,48},{32,0},{48,16},{1,33},{17,49},{33,1},{49,17},{2,34}... | collective-permute-start | bytes 688136 | tf_op jit(solution)/shard_map/ppermute | solution.py:201
  95.7 17.0 %collective-permute-start.6 = (bf16[224,512]{1,0:T(8,128)(2,1)S(1)}, bf16[224,512]{1,0:T(8,128)(2,1)S(1)}, u32[]{:S(2)}, u32[]{:S(2)}) collective-permute-start(bf16[224,512]{1,0:T(8,128)(2,1)S(1)} %get-tuple-element.13), channel_id=1, source_target_pairs={{0,48},{16,0},{32,16},{48,32},{1,49},{17,1},{33,17},{49,33},{2,50}... | collective-permute-start | bytes 688136 | tf_op jit(solution)/shard_map/ppermute | solution.py:201
  100.2 12.4 %collective-permute-start.5 = (bf16[224,512]{1,0:T(8,128)(2,1)S(1)}, bf16[224,512]{1,0:T(8,128)(2,1)S(1)}, u32[]{:S(2)}, u32[]{:S(2)}) collective-permute-start(bf16[224,512]{1,0:T(8,128)(2,1)S(1)} %get-tuple-element.12), channel_id=1, source_target_pairs={{0,16},{16,32},{32,48},{48,0},{1,17},{17,33},{33,49},{49,1},{2,18}... | collective-permute-start | bytes 688136 | tf_op jit(solution)/shard_map/ppermute | solution.py:201
  106.9 17.7 %collective-permute-start.12 = (bf16[224,1024]{1,0:T(8,128)(2,1)S(1)}, bf16[224,1024]{1,0:T(8,128)(2,1)S(1)}, u32[]{:S(2)}, u32[]{:S(2)}) collective-permute-start(bf16[224,1024]{1,0:T(8,128)(2,1)S(1)} %shard_map.73), channel_id=1, source_target_pairs={{0,0},{16,176},{32,288},{48,400},{64,64},{80,240},{96,352},{112,46... | collective-permute-start | bytes 1376264 | tf_op jit(solution)/shard_map/ppermute | solution.py:193
